TPU v7x, 32 devices: a whole 2x2x4 slice. The times are simulated.
32 devices in a mesh: space: 8 (over y, x, core), rep: 4 (over z).
Axes of the slice: x: 2, y: 2, z: 4, core: 2. Of those that a mesh axis runs over, the one named last changes fastest.
Arguments:
- leaf_density: bfloat16 [888, 8192], P(None, 'space'), may hold values from -6 to 6
- upward_ops: bfloat16 [8, 888, 888], P(None, 'rep'), may hold values from -0.0625 to 0.0625
- far_ops: bfloat16 [12, 888, 888], P('rep'), may hold values from -0.0625 to 0.0625
- downward_ops: bfloat16 [8, 888, 888], P(None, 'rep'), may hold values from -0.1875 to 0.1875
- fine_lists: int32 [12, 8192], P('rep', 'space'), may hold values from 0 to 3071
- coarse_lists: int32 [12, 1024], P('rep', 'space'), may hold values from 0 to 383
Outputs:
- local_check: bfloat16 [888, 8192], P('rep', 'space')
Inputs may be any that keep to these rules, and one draw needn't show every extreme that they name: `fine_lists`: entry k of box g names a box of the previous subtree (below 1024), of its own (below 2048) or of the next one; indices outside the grid of subtrees read zeros. `coarse_lists`: entry k of coarse box p names a coarse box of the previous coarse subtree (below 128), of its own (below 256) or of the next one; indices outside the grid read zeros.
All inputs are finite; a program needn't handle non-finite values.
Results may differ from a plain program's by a relative error of at most 0.013.
Values may be sent and summed in bfloat16 or wider, within the bound.
A program may use at most 128 MiB of HBM per device.

v0:
```python
import jax
import jax.numpy as jnp
from jax import lax
from jax.sharding import PartitionSpec as P

coarse_scale = 0.5


def extended(x, sides, width):
    for axis, dim in sides:
        peers, length = (lax.axis_size(axis), x.shape[dim])
        up = [(i, (i + 1) % peers) for i in range(peers - 1)]
        down = [(j, i) for i, j in up]
        last = lax.slice_in_dim(x, length - width, length, axis=dim)
        initial = lax.slice_in_dim(x, 0, width, axis=dim)
        before = lax.ppermute(last, axis, up)
        after = lax.ppermute(initial, axis, down)
        x = jnp.concatenate([before, x, after], axis=dim)
    return x


def parent_rows(leaf_density, upward_ops):
    density_rows, box_count = leaf_density.shape
    children = leaf_density.reshape(density_rows, box_count // 8, 8)
    parents = jnp.einsum("crq,qpc->rp", upward_ops, children, preferred_element_type=jnp.float32)
    return parents.astype(jnp.bfloat16)


def translate(operators, sources, lists):
    summed = jnp.zeros((operators.shape[1], lists.shape[1]), jnp.float32)
    for offset in range(operators.shape[0]):
        picked = jnp.take(sources, lists[offset], axis=1)
        summed = summed + jnp.dot(operators[offset], picked, preferred_element_type=jnp.float32)
    return summed


def local(leaf_density, upward_ops, far_ops, downward_ops, fine_lists, coarse_lists):
    up_rows = parent_rows(leaf_density, upward_ops)
    coarse_width = up_rows.shape[1]
    stacked = lax.all_gather(up_rows, "rep", axis=0, tiled=True)
    coarse_window = extended(stacked, (("space", 1),), coarse_width)
    window = extended(leaf_density, (("space", 1),), leaf_density.shape[1])
    fine_partial = translate(far_ops, window, fine_lists)
    coarse_partial = coarse_scale * translate(far_ops, coarse_window, coarse_lists)
    fine_check = lax.psum_scatter(
        fine_partial.astype(jnp.bfloat16), "rep", scatter_dimension=0, tiled=True
    ).astype(jnp.float32)
    coarse_check = lax.psum(coarse_partial.astype(jnp.bfloat16), "rep")
    parents_here = coarse_check.shape[1]
    spread = jnp.einsum(
        "crq,qp->rpc", downward_ops, coarse_check, preferred_element_type=jnp.float32
    )
    return (fine_check + spread.reshape(spread.shape[0], parents_here * 8)).astype(jnp.bfloat16)


def solution(mesh):
    return jax.shard_map(
        local,
        mesh=mesh,
        in_specs=(
            P(None, "space"),
            P(None, "rep", None),
            P("rep", None, None),
            P(None, "rep", None),
            P("rep", "space"),
            P("rep", "space"),
        ),
        out_specs=P("rep", "space"),
        check_vma=False,
    )
```

profile of v0, /device:TPU:3, one launch (start us, length us, event | category | flops | bytes accessed | tf_op | source)
XLA Modules:
  0.0 189.9 jit_solution(11422318837197953695)
XLA Ops:
  6.5 0.0 copy-start
  6.5 0.0 all-reduce.4.cloned.1.call-start
  6.5 3.9 %collective-permute-start = (bf16[888,1024]{1,0:T(8,128)(2,1)}, bf16[888,1024]{1,0:T(8,128)(2,1)}, u32[]{:S(2)}, u32[]{:S(2)}) collective-permute-start(bf16[888,1024]{1,0:T(8,128)(2,1)} %param.10), channel_id=1, source_target_pairs={{0,4},{4,8},{8,12},{12,16},{16,20},{20,24},{24,28},{1,5},{5,9},{9,... | collective-permute-start | bytes 5455880 | tf_op jit(solution)/shard_map/ppermute | solution.py:16
  10.5 1.9 %collective-permute-start.1 = (bf16[888,1024]{1,0:T(8,128)(2,1)}, bf16[888,1024]{1,0:T(8,128)(2,1)}, u32[]{:S(2)}, u32[]{:S(2)}) collective-permute-start(bf16[888,1024]{1,0:T(8,128)(2,1)} %param.10), channel_id=1, source_target_pairs={{4,0},{8,4},{12,8},{16,12},{20,16},{24,20},{28,24},{5,1},{9,5},{13... | collective-permute-start | bytes 5455880 | tf_op jit(solution)/shard_map/ppermute | solution.py:17
  12.4 3.8 %copy.43 = bf16[888,1024]{0,1:T(8,128)(2,1)} copy(bf16[888,1024]{1,0:T(8,128)(2,1)} %param.10) | data formatting | bytes 3637248 | tf_op args[0]
  16.2 3.5 %fusion.66 = bf16[1,222,128]{2,1,0:T(8,128)(2,1)S(1)} fusion(bf16[888,128,8]{0,2,1:T(8,128)(2,1)} %bitcast.81, bf16[8,222,888]{2,0,1:T(8,128)(2,1)} %param.11), kind=kOutput, calls=%fused_computation.49 | convolution fusion | flops 403762944 | bytes 5029632 | tf_op jit(solution)/shard_map/crq,qpc->rp/dot_general | solution.py:25
  19.7 12.3 %all-gather = bf16[4,222,128]{2,1,0:T(8,128)(2,1)S(1)} all-gather(bf16[1,222,128]{2,1,0:T(8,128)(2,1)S(1)} %fusion.66), channel_id=1, replica_groups=mesh['space'=8,'rep'=4] {'rep'}, dimensions={0}, use_global_device_ids=true | all-gather | bytes 284160 | tf_op jit(solution)/shard_map/all_gather | solution.py:40
  32.0 0.8 reshape.73
  32.8 1.1 copy.48
  33.8 4.3 %collective-permute-start.3 = (bf16[888,128]{0,1:T(8,128)(2,1)S(1)}, bf16[888,128]{0,1:T(8,128)(2,1)}, u32[]{:S(2)}, u32[]{:S(2)}) collective-permute-start(bf16[888,128]{0,1:T(8,128)(2,1)S(1)} %copy.48), channel_id=1, source_target_pairs={{4,0},{8,4},{12,8},{16,12},{20,16},{24,20},{28,24},{5,1},{9,5},{13... | collective-permute-start | bytes 681992 | tf_op jit(solution)/shard_map/ppermute | solution.py:17
  38.1 3.8 %collective-permute-start.2 = (bf16[888,128]{0,1:T(8,128)(2,1)S(1)}, bf16[888,128]{0,1:T(8,128)(2,1)}, u32[]{:S(2)}, u32[]{:S(2)}) collective-permute-start(bf16[888,128]{0,1:T(8,128)(2,1)S(1)} %copy.48), channel_id=1, source_target_pairs={{0,4},{4,8},{8,12},{12,16},{16,20},{20,24},{24,28},{1,5},{5,9},{9,... | collective-permute-start | bytes 681992 | tf_op jit(solution)/shard_map/ppermute | solution.py:16
  42.0 0.0 copy-done.5
  42.0 0.0 copy-done.4
  42.1 0.0 copy-done.6
  42.2 0.6 dynamic-slice.4
  43.4 13.4 %collective-permute-done.3 = bf16[888,128]{0,1:T(8,128)(2,1)} collective-permute-done((bf16[888,128]{0,1:T(8,128)(2,1)S(1)}, bf16[888,128]{0,1:T(8,128)(2,1)}, u32[]{:S(2)}, u32[]{:S(2)}) %collective-permute-start.3) | collective-permute-done | bytes 227360 | tf_op jit(solution)/shard_map/ppermute | solution.py:17
  56.8 0.0 collective-permute-done.2
  56.8 2.0 %pad_maximum_fusion.1 = bf16[888,384]{0,1:T(8,128)(2,1)} fusion(bf16[888,128]{0,1:T(8,128)(2,1)} %collective-permute-done.3, bf16[888,128]{0,1:T(8,128)(2,1)S(1)} %copy.48, bf16[888,128]{0,1:T(8,128)(2,1)} %collective-permute-done.2), kind=kLoop, calls=%fused_computation.54 | loop fusion | flops 2045952 | bytes 1363968 | tf_op jit(solution)/shard_map/concatenate | solution.py:18
  58.8 2.9 %gather_fusion.5 = bf16[128,888]{1,0:T(8,128)(2,1)} fusion(bf16[888,384]{0,1:T(8,128)(2,1)} %pad_maximum_fusion.1, s32[1024]{0:T(1024)S(1)} %get-tuple-element.20), kind=kCustom, calls=%fused_computation.5.clone | custom fusion | bytes 455168 | tf_op jit(solution)/shard_map/jit(_take)/gather | solution.py:32
  61.7 2.9 %gather_fusion.4 = bf16[128,888]{1,0:T(8,128)(2,1)} fusion(bf16[888,384]{0,1:T(8,128)(2,1)} %pad_maximum_fusion.1, s32[1024]{0:T(1024)S(1)} %get-tuple-element.21), kind=kCustom, calls=%fused_computation.4.clone | custom fusion | bytes 455168 | tf_op jit(solution)/shard_map/jit(_take)/gather | solution.py:32
  64.6 2.2 %gather_fusion.3 = bf16[128,888]{1,0:T(8,128)(2,1)S(1)} fusion(bf16[888,384]{0,1:T(8,128)(2,1)} %pad_maximum_fusion.1, s32[1024]{0:T(1024)S(1)} %pad_clamp_fusion.2), kind=kCustom, calls=%fused_computation.1.clone | custom fusion | bytes 455168 | tf_op jit(solution)/shard_map/jit(_take)/gather | solution.py:32
  66.8 0.0 copy-start.3
  66.8 2.3 %fusion.19 = f32[128,888]{0,1:T(8,128)S(1)} fusion(bf16[3,888,888]{2,1,0:T(8,128)(2,1)} %param.12, bf16[128,888]{1,0:T(8,128)(2,1)} %gather_fusion.5, pred[128]{0:T(512)(128)(4,1)S(1)} %get-tuple-element.16), kind=kOutput, calls=%fused_computation.26 | convolution fusion | flops 201980928 | bytes 2275456 | tf_op jit(solution)/shard_map/dot_general | solution.py:33
  69.1 0.0 copy-done.3
  69.1 2.1 %fusion.22 = f32[128,888]{0,1:T(8,128)S(1)} fusion(bf16[3,888,888]{2,1,0:T(8,128)(2,1)} %param.12, bf16[128,888]{1,0:T(8,128)(2,1)S(1)} %copy-done.3, pred[128]{0:T(512)(128)(4,1)S(1)} %get-tuple-element.18), kind=kOutput, calls=%fused_computation.29 | convolution fusion | flops 201980928 | bytes 2273408 | tf_op jit(solution)/shard_map/dot_general | solution.py:33
  71.2 2.9 %fusion.53 = bf16[888,128]{1,0:T(8,128)(2,1)} fusion(f32[128,888]{0,1:T(8,128)S(1)} %fusion.19, f32[128,888]{0,1:T(8,128)S(1)} %fusion.22, bf16[3,888,888]{2,1,0:T(8,128)(2,1)} %param.12, bf16[128,888]{1,0:T(8,128)(2,1)S(1)} %gather_fusion.3, pred[128]{0:T(512)(128)(4,1)S(1)} %get-tuple-element.6), kind=kOutput, calls=%fused_computation.46 | convolution fusion | flops 202435584 | bytes 2955392 | tf_op jit(solution)/shard_map/dot_general | solution.py:33
  74.0 0.0 all-reduce.4.cloned.1.call-update
  74.1 0.0 collective-permute-done
  74.1 4.0 %copy.42 = bf16[888,1024]{0,1:T(8,128)(2,1)} copy(bf16[888,1024]{1,0:T(8,128)(2,1)} %collective-permute-done) | data formatting | bytes 3637248 | tf_op jit(solution)/shard_map/ppermute | solution.py:16
  78.1 0.0 collective-permute-done.1
  78.1 3.8 %copy.44 = bf16[888,1024]{0,1:T(8,128)(2,1)} copy(bf16[888,1024]{1,0:T(8,128)(2,1)} %collective-permute-done.1) | data formatting | bytes 3637248 | tf_op jit(solution)/shard_map/ppermute | solution.py:17
  82.0 5.5 %pad_maximum_fusion = bf16[888,3072]{0,1:T(8,128)(2,1)} fusion(bf16[888,1024]{0,1:T(8,128)(2,1)} %copy.44, bf16[888,1024]{0,1:T(8,128)(2,1)} %copy.43, bf16[888,1024]{0,1:T(8,128)(2,1)} %copy.42), kind=kLoop, calls=%fused_computation.6 | loop fusion | flops 16367616 | bytes 10911744 | tf_op jit(solution)/shard_map/concatenate | solution.py:18
  87.5 9.1 %gather_fusion.2 = bf16[1024,888]{1,0:T(8,128)(2,1)} fusion(bf16[888,3072]{0,1:T(8,128)(2,1)} %pad_maximum_fusion, s32[1024]{0:T(1024)S(1)} %fusion.89), kind=kCustom, calls=%fused_computation.3.clone | custom fusion | bytes 3641344 | tf_op jit(solution)/shard_map/jit(_take)/gather | solution.py:32
  96.5 9.1 %gather_fusion.1 = bf16[1024,888]{1,0:T(8,128)(2,1)} fusion(bf16[888,3072]{0,1:T(8,128)(2,1)} %pad_maximum_fusion, s32[1024]{0:T(1024)S(1)} %fusion.88), kind=kCustom, calls=%fused_computation.2.clone | custom fusion | bytes 3641344 | tf_op jit(solution)/shard_map/jit(_take)/gather | solution.py:32
  105.6 9.0 %gather_fusion = bf16[1024,888]{1,0:T(8,128)(2,1)} fusion(bf16[888,3072]{0,1:T(8,128)(2,1)} %pad_maximum_fusion, s32[1024]{0:T(1024)S(1)} %fusion.87), kind=kCustom, calls=%fused_computation.clone | custom fusion | bytes 3641344 | tf_op jit(solution)/shard_map/jit(_take)/gather | solution.py:32
  114.7 4.3 %fusion.9 = f32[1024,888]{0,1:T(8,128)S(1)} fusion(bf16[1024,888]{1,0:T(8,128)(2,1)} %gather_fusion, pred[1024]{0:T(1024)(128)(4,1)S(1)} %compare_and_fusion.2, bf16[3,888,888]{2,1,0:T(8,128)(2,1)} %param.12), kind=kOutput, calls=%fused_computation.16 | convolution fusion | flops 1615847424 | bytes 7064576 | tf_op jit(solution)/shard_map/dot_general | solution.py:33
  119.0 3.8 %fusion.7 = f32[1024,888]{0,1:T(8,128)S(1)} fusion(bf16[1024,888]{1,0:T(8,128)(2,1)S(1)} %copy-done.2, pred[1024]{0:T(1024)(128)(4,1)S(1)} %compare_and_fusion.1, bf16[3,888,888]{2,1,0:T(8,128)(2,1)} %param.12), kind=kOutput, calls=%fused_computation.14 | convolution fusion | flops 1615847424 | bytes 7048192 | tf_op jit(solution)/shard_map/dot_general | solution.py:33
  122.8 4.9 %fusion.18 = bf16[888,1024]{1,0:T(8,128)(2,1)} fusion(f32[1024,888]{0,1:T(8,128)S(1)} %fusion.9, f32[1024,888]{0,1:T(8,128)S(1)} %fusion.7, bf16[3,888,888]{2,1,0:T(8,128)(2,1)} %param.12, bf16[1024,888]{1,0:T(8,128)(2,1)S(1)} %copy-done.1, pred[1024]{0:T(1024)(128)(4,1)S(1)} %compare_and_fusion), kind=kOutput, calls=%fused_computation.25 | convolution fusion | flops 1618575360 | bytes 12504064 | tf_op jit(solution)/shard_map/dot_general | solution.py:33
  127.7 39.2 %fusion = bf16[224,1024]{1,0:T(8,128)(2,1)} fusion(bf16[888,1024]{1,0:T(8,128)(2,1)} %fusion.18), kind=kCustom, calls=%all-reduce-scatter | all-reduce-scatter fusion | flops 917505 | bytes 2277888
  166.9 0.7 slice.51
  167.6 1.3 collective-permute-start.4
  168.9 0.0 all-reduce.4.cloned.1.call-done
  168.9 2.9 %fusion.38 = f32[222,128,8]{1,0,2:T(8,128)} fusion(bf16[8,222,888]{2,0,1:T(8,128)(2,1)S(1)} %copy-done, bf16[888,128]{1,0:T(8,128)(2,1)} %all-reduce.4.cloned.1.call-done), kind=kOutput, calls=%fused_computation.41 | convolution fusion | flops 403734528 | bytes 4290816 | tf_op jit(solution)/shard_map/crq,qp->rpc/dot_general | solution.py:50
  171.8 2.6 %copy.52 = f32[222,128,8]{0,2,1:T(8,128)} copy(f32[222,128,8]{1,0,2:T(8,128)} %fusion.38) | data formatting | bytes 1818624 | tf_op jit(solution)/shard_map/crq,qp->rpc/transpose | solution.py:50
  174.4 2.5 %copy.53 = f32[222,1024]{1,0:T(8,128)} copy(f32[222,1024]{0,1:T(8,128)} %bitcast.82) | data formatting | bytes 1818624 | tf_op jit(solution)/shard_map/reshape | solution.py:53
  176.9 0.0 collective-permute-done.4
  176.9 3.9 %concatenate.8 = bf16[230,1024]{1,0:T(8,128)(2,1)} concatenate(bf16[6,1024]{1,0:T(8,128)(2,1)S(1)} %collective-permute-done.4, bf16[224,1024]{1,0:T(8,128)(2,1)} %fusion), dimensions={0} | concatenate | bytes 942080
  180.8 2.2 %add_convert_fusion.1 = bf16[222,1024]{1,0:T(8,128)(2,1)} fusion(f32[222,1024]{1,0:T(8,128)} %copy.53, bf16[230,1024]{1,0:T(8,128)(2,1)} %concatenate.8, u32[]{:S(6)} %subtract), kind=kLoop, calls=%fused_computation.53 | loop fusion | flops 681984 | bytes 1818628 | tf_op jit(solution)/shard_map/convert_element_type | solution.py:53
  (18 shorter events, 0.1 us)
Async XLA Ops:
  6.5 162.4 %copy-start = (bf16[8,222,888]{2,0,1:T(8,128)(2,1)S(1)}, bf16[8,222,888]{2,0,1:T(8,128)(2,1)}, u32[]{:S(2)}) copy-start(bf16[8,222,888]{2,0,1:T(8,128)(2,1)} %param.13) | copy-start | bytes 9462532
  6.5 162.4 %all-reduce.4.cloned.1.call-start = ((), (), s32[]{:S(2)}) async-start(), calls=%async_computation | async-start | bytes 454656 | tf_op jit(solution)/shard_map/psum | solution.py:48
  6.5 67.5 %collective-permute-start = (bf16[888,1024]{1,0:T(8,128)(2,1)}, bf16[888,1024]{1,0:T(8,128)(2,1)}, u32[]{:S(2)}, u32[]{:S(2)}) collective-permute-start(bf16[888,1024]{1,0:T(8,128)(2,1)} %param.10), channel_id=1, source_target_pairs={{0,4},{4,8},{8,12},{12,16},{16,20},{20,24},{24,28},{1,5},{5,9},{9,... | collective-permute-start | bytes 5455880 | tf_op jit(solution)/shard_map/ppermute | solution.py:16
  10.5 67.7 %collective-permute-start.1 = (bf16[888,1024]{1,0:T(8,128)(2,1)}, bf16[888,1024]{1,0:T(8,128)(2,1)}, u32[]{:S(2)}, u32[]{:S(2)}) collective-permute-start(bf16[888,1024]{1,0:T(8,128)(2,1)} %param.10), channel_id=1, source_target_pairs={{4,0},{8,4},{12,8},{16,12},{20,16},{24,20},{28,24},{5,1},{9,5},{13... | collective-permute-start | bytes 5455880 | tf_op jit(solution)/shard_map/ppermute | solution.py:17
  16.2 25.8 %copy-start.5 = (s32[3,128]{1,0:T(4,128)S(1)}, s32[3,128]{1,0:T(4,128)}, u32[]{:S(2)}) copy-start(s32[3,128]{1,0:T(4,128)} %param.15) | copy-start | bytes 4612
  16.2 25.8 %copy-start.4 = (s32[3,1024]{1,0:T(4,128)S(1)}, s32[3,1024]{1,0:T(4,128)}, u32[]{:S(2)}) copy-start(s32[3,1024]{1,0:T(4,128)} %param.14) | copy-start | bytes 36868
  16.2 25.9 %copy-start.6 = (u32[32]{0:T(128)S(1)}, u32[32]{0:T(128)}, u32[]{:S(2)}) copy-start(u32[32]{0:T(128)} %constant.29) | copy-start | bytes 388
  33.8 23.0 %collective-permute-start.3 = (bf16[888,128]{0,1:T(8,128)(2,1)S(1)}, bf16[888,128]{0,1:T(8,128)(2,1)}, u32[]{:S(2)}, u32[]{:S(2)}) collective-permute-start(bf16[888,128]{0,1:T(8,128)(2,1)S(1)} %copy.48), channel_id=1, source_target_pairs={{4,0},{8,4},{12,8},{16,12},{20,16},{24,20},{28,24},{5,1},{9,5},{13... | collective-permute-start | bytes 681992 | tf_op jit(solution)/shard_map/ppermute | solution.py:17
  38.1 18.7 %collective-permute-start.2 = (bf16[888,128]{0,1:T(8,128)(2,1)S(1)}, bf16[888,128]{0,1:T(8,128)(2,1)}, u32[]{:S(2)}, u32[]{:S(2)}) collective-permute-start(bf16[888,128]{0,1:T(8,128)(2,1)S(1)} %copy.48), channel_id=1, source_target_pairs={{0,4},{4,8},{8,12},{12,16},{16,20},{20,24},{24,28},{1,5},{5,9},{9,... | collective-permute-start | bytes 681992 | tf_op jit(solution)/shard_map/ppermute | solution.py:16
  66.8 2.3 %copy-start.3 = (bf16[128,888]{1,0:T(8,128)(2,1)S(1)}, bf16[128,888]{1,0:T(8,128)(2,1)}, u32[]{:S(2)}) copy-start(bf16[128,888]{1,0:T(8,128)(2,1)} %gather_fusion.4) | copy-start | bytes 681988
  114.7 4.3 %copy-start.2 = (bf16[1024,888]{1,0:T(8,128)(2,1)S(1)}, bf16[1024,888]{1,0:T(8,128)(2,1)}, u32[]{:S(2)}) copy-start(bf16[1024,888]{1,0:T(8,128)(2,1)} %gather_fusion.1) | copy-start | bytes 5455876
  119.0 3.8 %copy-start.1 = (bf16[1024,888]{1,0:T(8,128)(2,1)S(1)}, bf16[1024,888]{1,0:T(8,128)(2,1)}, u32[]{:S(2)}) copy-start(bf16[1024,888]{1,0:T(8,128)(2,1)} %gather_fusion.2) | copy-start | bytes 5455876
  167.6 9.3 %collective-permute-start.4 = (bf16[6,1024]{1,0:T(8,128)(2,1)S(1)}, bf16[6,1024]{1,0:T(8,128)(2,1)S(1)}, u32[]{:S(2)}, u32[]{:S(2)}) collective-permute-start(bf16[6,1024]{1,0:T(8,128)(2,1)S(1)} %slice.51), channel_id=1, source_target_pairs={{0,1},{1,2},{2,3},{4,5},{5,6},{6,7},{8,9},{9,10},{10,11},{12,13},{... | collective-permute-start | bytes 36872
Sparse Core Ops, SparseCore 0:
  74.2 33.0 all-reduce.3
where the time goes:
time: 191 us; the launch traced here: 190 us
  local copies, waits for them, and re-layouts  59 us (31%)
  blocking collectives  51.4 us (27%)
  matrix products  26.6 us (14%)
  starting transfers between devices  15.3 us (8%)
  between operations  14.3 us (7%)
  waiting for transfers between devices  13.5 us (7%)
  other arithmetic  9.75 us (5%)
    unnamed x1, blocking collectives  39.2 us
    gather x6, local copies, waits for them, and re-layouts, translate(): picked = jnp.take(sources, lists[offset], axis=1)  35.2 us
    dot_general x6, matrix products, translate(): jnp.dot(operators[offset], picked, preferred_element_type=jnp.float32)  20.2 us
    ppermute x2, waiting for transfers between devices, extended(): after = lax.ppermute(initial, axis, down)  13.4 us
    all_gather x1, blocking collectives, local(): stacked = lax.all_gather(up_rows, 'rep', axis=0, tiled=True)  12.3 us
    unnamed x20, local copies, waits for them, and re-layouts  10.9 us
    ppermute x2, starting transfers between devices, extended(): before = lax.ppermute(last, axis, up)  7.78 us
    concatenate x2, other arithmetic, extended(): x = jnp.concatenate([before, x, after], axis=dim)  7.46 us
  transfers between devices with their start and end apart: 6, of which 1 were waited for; matrix products, arithmetic and copies ran while one was open for 68% of the time, Pallas kernels for 0%

commit v1 on v0

v1 whole, which is shorter than its diff:
```python
import functools

import jax
import jax.numpy as jnp
from jax import lax
from jax.experimental import pallas as pl
from jax.experimental.pallas import tpu as pltpu
from jax.sharding import PartitionSpec as P

coarse_scale = 0.5
F32, BF16 = jnp.float32, jnp.bfloat16
VM = pltpu.VMEM
PARAMS = pltpu.CompilerParams(vmem_limit_bytes=48 * 2**20)


def whole(count):
    return [pl.BlockSpec(memory_space=VM) for _ in range(count)]


def dot(a, b):
    return jnp.dot(a, b, preferred_element_type=F32)


def one_hot(row, first, count):
    spots = lax.broadcasted_iota(jnp.int32, (count, row.shape[1]), 0) + first
    return jnp.where(spots == row, 1.0, 0.0).astype(BF16)


def upward_kernel(density, ops, out):
    children, parents = ops.shape[0], out.shape[1]
    boxes = density.shape[1]
    total = jnp.zeros(out.shape, F32)
    for child in range(children):
        box = lax.broadcasted_iota(jnp.int32, (boxes, parents), 0)
        parent = lax.broadcasted_iota(jnp.int32, (boxes, parents), 1)
        pick = jnp.where(box == parent * children + child, 1.0, 0.0).astype(BF16)
        total += dot(ops[child], dot(density[...], pick).astype(BF16))
    out[...] = total.astype(BF16)


def own_kernel(lists, density, out):
    boxes = density.shape[1]
    out[...] = dot(density[...], one_hot(lists[0], boxes, boxes)).astype(BF16)


def far_kernel(lists, before, after, picked, ops, out):
    boxes = before.shape[1]
    total = jnp.zeros((ops.shape[1], out.shape[2]), F32)
    for entry in range(ops.shape[0]):
        row = lists[entry]
        sources = picked[entry].astype(F32)
        sources += dot(before[...], one_hot(row, 0, boxes))
        sources += dot(after[...], one_hot(row, 2 * boxes, boxes))
        total += dot(ops[entry], sources.astype(BF16))
    block = out.shape[1]
    for owner in range(out.shape[0]):
        out[owner] = total[owner * block:(owner + 1) * block].astype(BF16)


def coarse_kernel(lists, before, own, after, ops, out):
    boxes = own.shape[1]
    total = jnp.zeros(out.shape, F32)
    for entry in range(ops.shape[0]):
        row = lists[entry]
        sources = dot(own[...], one_hot(row, boxes, boxes))
        sources += dot(before[...], one_hot(row, 0, boxes))
        sources += dot(after[...], one_hot(row, 2 * boxes, boxes))
        total += dot(ops[entry], sources.astype(BF16))
    out[...] = (coarse_scale * total).astype(BF16)


def downward_kernel(check, ops, fine, out):
    children, parents = ops.shape[0], check.shape[1]
    boxes = out.shape[1]
    total = fine[...].astype(F32)
    for child in range(children):
        term = dot(ops[child], check[...])
        high = term.astype(BF16)
        low = (term - high.astype(F32)).astype(BF16)
        parent = lax.broadcasted_iota(jnp.int32, (parents, boxes), 0)
        box = lax.broadcasted_iota(jnp.int32, (parents, boxes), 1)
        place = jnp.where(box == parent * children + child, 1.0, 0.0).astype(BF16)
        total += dot(high, place) + dot(low, place)
    out[...] = total.astype(BF16)


def local(leaf_density, upward_ops, far_ops, downward_ops, fine_lists, coarse_lists):
    rows, boxes = leaf_density.shape
    children, own_rows, _ = upward_ops.shape
    parents = boxes // children
    slots = far_ops.shape[0]
    wide = 256 if boxes % 256 == 0 else boxes
    peers = lax.axis_size("space")
    up = [(i, i + 1) for i in range(peers - 1)]
    down = [(j, i) for i, j in up]
    before = lax.ppermute(leaf_density, "space", up)
    after = lax.ppermute(leaf_density, "space", down)
    fine3 = fine_lists.reshape(slots, 1, boxes)
    coarse3 = coarse_lists.reshape(slots, 1, parents)

    up_rows = pl.pallas_call(
        upward_kernel,
        out_shape=jax.ShapeDtypeStruct((own_rows, parents), BF16),
        in_specs=whole(2), out_specs=whole(1)[0], compiler_params=PARAMS,
        cost_estimate=pl.CostEstimate(
            flops=2 * rows * boxes * (boxes + own_rows), bytes_accessed=6 * 2**20, transcendentals=0),
    )(leaf_density, upward_ops)
    stacked = lax.all_gather(up_rows, "rep", axis=0, tiled=True)
    coarse_before = lax.ppermute(stacked, "space", up)
    coarse_after = lax.ppermute(stacked, "space", down)

    picked = pl.pallas_call(
        own_kernel,
        grid=(slots, boxes // wide),
        out_shape=jax.ShapeDtypeStruct((slots, rows, boxes), BF16),
        in_specs=[
            pl.BlockSpec((1, 1, wide), lambda k, c: (k, 0, c)),
            pl.BlockSpec((rows, boxes), lambda k, c: (0, 0)),
        ],
        out_specs=pl.BlockSpec((None, rows, wide), lambda k, c: (k, 0, c)),
        compiler_params=PARAMS,
        cost_estimate=pl.CostEstimate(
            flops=2 * rows * boxes * boxes * slots, bytes_accessed=8 * 2**20, transcendentals=0),
    )(fine3, leaf_density)

    coarse_partial = pl.pallas_call(
        coarse_kernel,
        out_shape=jax.ShapeDtypeStruct((rows, parents), BF16),
        in_specs=whole(5), out_specs=whole(1)[0], compiler_params=PARAMS,
        cost_estimate=pl.CostEstimate(
            flops=2 * rows * parents * slots * (3 * parents + rows),
            bytes_accessed=6 * 2**20, transcendentals=0),
    )(coarse3, coarse_before, stacked, coarse_after, far_ops)
    coarse_check = lax.psum(coarse_partial, "rep")

    fine_partial = pl.pallas_call(
        far_kernel,
        grid=(boxes // wide,),
        out_shape=jax.ShapeDtypeStruct((rows // own_rows, own_rows, boxes), BF16),
        in_specs=[
            pl.BlockSpec((slots, 1, wide), lambda c: (0, 0, c)),
            pl.BlockSpec((rows, boxes), lambda c: (0, 0)),
            pl.BlockSpec((rows, boxes), lambda c: (0, 0)),
            pl.BlockSpec((slots, rows, wide), lambda c: (0, 0, c)),
            pl.BlockSpec((slots, rows, rows), lambda c: (0, 0, 0)),
        ],
        out_specs=pl.BlockSpec((rows // own_rows, own_rows, wide), lambda c: (0, 0, c)),
        compiler_params=PARAMS,
        cost_estimate=pl.CostEstimate(
            flops=2 * rows * boxes * slots * (2 * boxes + rows),
            bytes_accessed=16 * 2**20, transcendentals=0),
    )(fine3, before, after, picked, far_ops)
    fine_check = lax.psum_scatter(fine_partial, "rep", scatter_dimension=0, tiled=False)

    return pl.pallas_call(
        downward_kernel,
        out_shape=jax.ShapeDtypeStruct((own_rows, boxes), BF16),
        in_specs=whole(3), out_specs=whole(1)[0], compiler_params=PARAMS,
    )(coarse_check, downward_ops, fine_check)


def solution(mesh):
    return jax.shard_map(
        local,
        mesh=mesh,
        in_specs=(
            P(None, "space"),
            P(None, "rep", None),
            P("rep", None, None),
            P(None, "rep", None),
            P("rep", "space"),
            P("rep", "space"),
        ),
        out_specs=P("rep", "space"),
        check_vma=False,
    )
```

time: 191 us -> 152 us (0.80)
  local copies, waits for them, and re-layouts: 59 us -> 6.66 us
  Pallas kernels: 0 us -> 51.6 us
  blocking collectives: 51.4 us -> 12.3 us
  waiting for transfers between devices: 13.5 us -> 51.3 us
  matrix products: 26.6 us -> 0 us
  other arithmetic: 9.75 us -> 0.01 us
    pallas_call x0 -> x5, Pallas kernels: none -> 51.6 us  [the longest x1 26.2 us: local(): pl.pallas_call(far_kernel, grid=(boxes // wide,), out_shape=jax.ShapeDtyp...]
    reduce_scatter x0 -> x1, waiting for transfers between devices: none -> 43.2 us  [local(): lax.psum_scatter(fine_partial, 'rep', scatter_dimension=0, tiled=False)]
    unnamed x1 -> x0, blocking collectives: 39.2 us -> none
    gather x6 -> x0, local copies, waits for them, and re-layouts: 35.2 us -> none  [translate(): picked = jnp.take(sources, lists[offset], axis=1)]
    dot_general x8 -> x0, matrix products: 26.6 us -> none  [the longest x6 20.2 us: translate(): jnp.dot(operators[offset], picked, preferred_element_type=jnp.float32)]
    ppermute x4, waiting for transfers between devices: 13.4 us -> 3.71 us  [the longest x1 3.7 us: local(): coarse_after = lax.ppermute(stacked, 'space', down)]
    ppermute x2 -> x0, local copies, waits for them, and re-layouts: 7.87 us -> none  [the longest x1 4.05 us: extended(): before = lax.ppermute(last, axis, up)]
    concatenate x2 -> x0, other arithmetic: 7.46 us -> none  [extended(): x = jnp.concatenate([before, x, after], axis=dim)]
  transfers between devices with their start and end apart: 6 -> 6, of which waited for: 1 -> 3; matrix products, arithmetic and copies ran while one was open for 68% -> 3% of each run, Pallas kernels for 0% -> 31%
where the time goes in v1:
time: 152 us; the launch traced here: 150 us
  Pallas kernels  51.6 us (34%)
  waiting for transfers between devices  51.3 us (34%)
  starting transfers between devices  14.2 us (9%)
  between operations  13.5 us (9%)
  blocking collectives  12.3 us (8%)
  local copies, waits for them, and re-layouts  6.66 us (4%)
    reduce_scatter x1, waiting for transfers between devices, local(): lax.psum_scatter(fine_partial, 'rep', scatter_dimension=0, tiled=False)  43.2 us
    pallas_call x1, Pallas kernels, local(): pl.pallas_call(far_kernel, grid=(boxes // wide,), out_shape=jax.ShapeDtyp...  26.2 us
    all_gather x1, blocking collectives, local(): stacked = lax.all_gather(up_rows, 'rep', axis=0, tiled=True)  12.3 us
    pallas_call x1, Pallas kernels, local(): pl.pallas_call(own_kernel, grid=(slots, boxes // wide), out_shape=jax.Sha...  9.43 us
    pallas_call x1, Pallas kernels, local(): pl.pallas_call(upward_kernel, out_shape=jax.ShapeDtypeStruct((own_rows, p...  8.12 us
    unnamed x17, local copies, waits for them, and re-layouts  6.65 us
    ppermute x1, starting transfers between devices, local(): coarse_before = lax.ppermute(stacked, 'space', up)  6.32 us
    pallas_call x1, Pallas kernels, local(): pl.pallas_call(downward_kernel, out_shape=jax.ShapeDtypeStruct((own_rows,...  4.59 us
  transfers between devices with their start and end apart: 6, of which 3 were waited for; matrix products, arithmetic and copies ran while one was open for 3% of the time, Pallas kernels for 31%

profile of v1, /device:TPU:3, one launch (start us, length us, event | category | flops | bytes accessed | tf_op | source)
XLA Modules:
  0.0 149.6 jit_solution(2807239787785183400)
XLA Ops:
  6.5 0.0 copy-start.2
  6.5 0.0 all-reduce.2.cloned.1.call-start
  6.5 3.8 %collective-permute-start.2 = (bf16[888,1024]{1,0:T(8,128)(2,1)}, bf16[888,1024]{1,0:T(8,128)(2,1)}, u32[]{:S(2)}, u32[]{:S(2)}) collective-permute-start(bf16[888,1024]{1,0:T(8,128)(2,1)} %density.3), channel_id=1, source_target_pairs={{0,4},{4,8},{8,12},{12,16},{16,20},{20,24},{24,28},{1,5},{5,9},{9,... | collective-permute-start | bytes 5455880 | tf_op jit(solution)/shard_map/ppermute | solution.py:96
  10.3 1.9 %collective-permute-start.3 = (bf16[888,1024]{1,0:T(8,128)(2,1)}, bf16[888,1024]{1,0:T(8,128)(2,1)}, u32[]{:S(2)}, u32[]{:S(2)}) collective-permute-start(bf16[888,1024]{1,0:T(8,128)(2,1)} %density.3), channel_id=1, source_target_pairs={{4,0},{8,4},{12,8},{16,12},{20,16},{24,20},{28,24},{5,1},{9,5},{13... | collective-permute-start | bytes 5455880 | tf_op jit(solution)/shard_map/ppermute | solution.py:97
  12.3 2.3 %copy.11.ops = bf16[8,222,888]{2,1,0:T(8,128)(2,1)S(1)} copy(bf16[8,222,888]{2,0,1:T(8,128)(2,1)} %param.7) | data formatting | bytes 6308352 | tf_op args[1]
  14.6 0.0 copy-done.2
  14.6 0.0 copy-start.3
  14.6 8.1 %shard_map.64 = bf16[222,128]{1,0:T(8,128)(2,1)S(1)} custom-call(bf16[888,1024]{1,0:T(8,128)(2,1)S(1)} %copy-done.2, bf16[8,222,888]{2,1,0:T(8,128)(2,1)S(1)} %copy.11.ops), custom_call_target="tpu_custom_call" | custom-call | flops 2266005504 | bytes 6291456 | tf_op jit(solution)/shard_map/pallas_call | solution.py:101
  22.7 12.3 %all-gather = bf16[4,222,128]{2,1,0:T(8,128)(2,1)S(1)} all-gather(bf16[1,222,128]{2,1,0:T(8,128)(2,1)S(1)} %bitcast.5), channel_id=1, replica_groups=mesh['space'=8,'rep'=4] {'rep'}, dimensions={0}, use_global_device_ids=true | all-gather | bytes 284160 | tf_op jit(solution)/shard_map/all_gather | solution.py:108
  35.0 0.0 slice-start
  35.0 0.1 reshape.9.own
  35.1 6.3 %collective-permute-start = (bf16[888,128]{1,0:T(8,128)(2,1)S(1)}, bf16[888,128]{1,0:T(8,128)(2,1)S(1)}, u32[]{:S(2)}, u32[]{:S(2)}) collective-permute-start(bf16[888,128]{1,0:T(8,128)(2,1)S(1)} %reshape.9.own), channel_id=1, source_target_pairs={{0,4},{4,8},{8,12},{12,16},{16,20},{20,24},{24,28},{1,5},{5,9},{9,... | collective-permute-start | bytes 681992 | tf_op jit(solution)/shard_map/ppermute | solution.py:109
  41.4 1.9 %collective-permute-start.1 = (bf16[888,128]{1,0:T(8,128)(2,1)S(1)}, bf16[888,128]{1,0:T(8,128)(2,1)S(1)}, u32[]{:S(2)}, u32[]{:S(2)}) collective-permute-start(bf16[888,128]{1,0:T(8,128)(2,1)S(1)} %reshape.9.own), channel_id=1, source_target_pairs={{4,0},{8,4},{12,8},{16,12},{20,16},{24,20},{28,24},{5,1},{9,5},{13... | collective-permute-start | bytes 681992 | tf_op jit(solution)/shard_map/ppermute | solution.py:110
  43.3 0.0 copy-done.3
  43.4 0.0 copy-start.4
  43.4 0.0 slice-start.1
  43.4 9.4 %shard_map.66.picked = bf16[3,888,1024]{2,1,0:T(8,128)(2,1)} custom-call(s32[3,1,1024]{2,1,0:T(1,128)S(1)} %reshape.7.lists, bf16[888,1024]{1,0:T(8,128)(2,1)S(1)} %copy-done.2), custom_call_target="tpu_custom_call" | custom-call | flops 5586812928 | bytes 8388608 | tf_op jit(solution)/shard_map/pallas_call | solution.py:112
  52.8 0.0 copy-done.4
  52.8 0.0 collective-permute-done.before
  52.8 3.7 %collective-permute-done.1.after = bf16[888,128]{1,0:T(8,128)(2,1)S(1)} collective-permute-done((bf16[888,128]{1,0:T(8,128)(2,1)S(1)}, bf16[888,128]{1,0:T(8,128)(2,1)S(1)}, u32[]{:S(2)}, u32[]{:S(2)}) %collective-permute-start.1) | collective-permute-done | bytes 227360 | tf_op jit(solution)/shard_map/ppermute | solution.py:110
  56.5 0.0 slice-done
  56.5 0.0 slice-done.1
  56.5 3.3 %shard_map.65 = bf16[888,128]{1,0:T(8,128)(2,1)} custom-call(s32[3,1,128]{2,1,0:T(1,128)S(1)} %reshape.6.lists, bf16[888,128]{1,0:T(8,128)(2,1)S(1)} %collective-permute-done.before, bf16[888,128]{1,0:T(8,128)(2,1)S(1)} %reshape.9.own, bf16[888,128]{1,0:T(8,128)(2,1)S(1)} %collective-permute-done.1.after, bf16[3,888,888]{2,1,0:T(8,128)(2,1)S(1)} %bitcast.3), custom_call_target="tpu_custom_call" | custom-call | flops 867483648 | bytes 6291456 | tf_op jit(solution)/shard_map/pallas_call | solution.py:126
  59.8 0.0 all-reduce.2.cloned.1.call-update
  59.9 0.2 reduce-scatter.2.cloned.1.call-start
  60.1 0.0 collective-permute-done.2.before
  60.1 0.0 collective-permute-done.3.after
  60.1 26.2 %shard_map.67 = bf16[4,222,1024]{2,1,0:T(8,128)(2,1)} custom-call(s32[3,1,1024]{2,1,0:T(1,128)S(1)} %reshape.7.lists, bf16[888,1024]{1,0:T(8,128)(2,1)} %collective-permute-done.2.before, bf16[888,1024]{1,0:T(8,128)(2,1)} %collective-permute-done.3.after, bf16[3,888,1024]{2,1,0:T(8,128)(2,1)} %shard_map.66.picked, bf16[3,888,888]{2,1,0:T(8,128)(2,1)} %ops.5), custom_call_target="tpu_custom_call" | custom-call | flops 16018440192 | bytes 16777216 | tf_op jit(solution)/shard_map/pallas_call | solution.py:136
  86.3 0.0 reduce-scatter.2.cloned.1.call-update
  86.3 2.3 %copy.12.ops = bf16[8,222,888]{2,1,0:T(8,128)(2,1)S(1)} copy(bf16[8,222,888]{2,0,1:T(8,128)(2,1)} %param.9) | data formatting | bytes 6308352 | tf_op args[3]
  88.6 4.4 %all-reduce.2.cloned.1.call-done.check = bf16[888,128]{1,0:T(8,128)(2,1)} async-done(((bf16[888,128]{1,0:T(8,128)(2,1)}), bf16[888,128]{1,0:T(8,128)(2,1)}) %all-reduce.2.cloned.1.call-update) | async-done | bytes 227344 | tf_op jit(solution)/shard_map/psum | solution.py:134
  93.0 43.2 %reduce-scatter.2.cloned.1.call-done = bf16[1,222,1024]{2,1,0:T(8,128)(2,1)} async-done(((bf16[4,222,1024]{2,1,0:T(8,128)(2,1)}), bf16[1,222,1024]{2,1,0:T(8,128)(2,1)}) %reduce-scatter.2.cloned.1.call-update) | async-done | bytes 454672 | tf_op jit(solution)/shard_map/reduce_scatter | solution.py:153
  136.2 0.0 copy-start
  136.2 1.0 copy-done
  137.2 0.0 copy-start.1
  137.2 0.9 copy-done.1
  138.1 4.6 %shard_map.68 = bf16[222,1024]{1,0:T(8,128)(2,1)} custom-call(bf16[888,128]{1,0:T(8,128)(2,1)S(1)} %copy-done.1, bf16[8,222,888]{2,1,0:T(8,128)(2,1)S(1)} %copy.12.ops, bf16[222,1024]{1,0:T(8,128)(2,1)S(1)} %bitcast.4), custom_call_target="tpu_custom_call" | custom-call | tf_op jit(solution)/shard_map/pallas_call | solution.py:155
  (3 shorter events, 0.0 us)
Async XLA Ops:
  6.5 8.0 %copy-start.2 = (bf16[888,1024]{1,0:T(8,128)(2,1)S(1)}, bf16[888,1024]{1,0:T(8,128)(2,1)}, u32[]{:S(2)}) copy-start(bf16[888,1024]{1,0:T(8,128)(2,1)} %density.3) | copy-start | bytes 5455876
  6.5 86.5 %all-reduce.2.cloned.1.call-start = ((), (), s32[]{:S(2)}) async-start(), calls=%async_computation.1 | async-start | bytes 454656 | tf_op jit(solution)/shard_map/psum | solution.py:134
  6.5 53.6 %collective-permute-start.2 = (bf16[888,1024]{1,0:T(8,128)(2,1)}, bf16[888,1024]{1,0:T(8,128)(2,1)}, u32[]{:S(2)}, u32[]{:S(2)}) collective-permute-start(bf16[888,1024]{1,0:T(8,128)(2,1)} %density.3), channel_id=1, source_target_pairs={{0,4},{4,8},{8,12},{12,16},{16,20},{20,24},{24,28},{1,5},{5,9},{9,... | collective-permute-start | bytes 5455880 | tf_op jit(solution)/shard_map/ppermute | solution.py:96
  10.3 49.8 %collective-permute-start.3 = (bf16[888,1024]{1,0:T(8,128)(2,1)}, bf16[888,1024]{1,0:T(8,128)(2,1)}, u32[]{:S(2)}, u32[]{:S(2)}) collective-permute-start(bf16[888,1024]{1,0:T(8,128)(2,1)} %density.3), channel_id=1, source_target_pairs={{4,0},{8,4},{12,8},{16,12},{20,16},{24,20},{28,24},{5,1},{9,5},{13... | collective-permute-start | bytes 5455880 | tf_op jit(solution)/shard_map/ppermute | solution.py:97
  14.6 28.8 %copy-start.3 = (s32[3,1024]{1,0:T(4,128)S(1)}, s32[3,1024]{1,0:T(4,128)}, u32[]{:S(2)}) copy-start(s32[3,1024]{1,0:T(4,128)} %param.10) | copy-start | bytes 36868
  35.0 21.5 %slice-start = ((s8[4773888]{0:T(1024)(128)(4,1)}), s8[579584]{0:T(1024)(128)(4,1)S(1)}, s32[]{:S(2)}) async-start(s8[4773888]{0:T(1024)(128)(4,1)} %bitcast.2), calls=%async_computation.3 | async-start | bytes 1159168
  35.1 17.8 %collective-permute-start = (bf16[888,128]{1,0:T(8,128)(2,1)S(1)}, bf16[888,128]{1,0:T(8,128)(2,1)S(1)}, u32[]{:S(2)}, u32[]{:S(2)}) collective-permute-start(bf16[888,128]{1,0:T(8,128)(2,1)S(1)} %reshape.9.own), channel_id=1, source_target_pairs={{0,4},{4,8},{8,12},{12,16},{16,20},{20,24},{24,28},{1,5},{5,9},{9,... | collective-permute-start | bytes 681992 | tf_op jit(solution)/shard_map/ppermute | solution.py:109
  41.4 15.1 %collective-permute-start.1 = (bf16[888,128]{1,0:T(8,128)(2,1)S(1)}, bf16[888,128]{1,0:T(8,128)(2,1)S(1)}, u32[]{:S(2)}, u32[]{:S(2)}) collective-permute-start(bf16[888,128]{1,0:T(8,128)(2,1)S(1)} %reshape.9.own), channel_id=1, source_target_pairs={{4,0},{8,4},{12,8},{16,12},{20,16},{24,20},{28,24},{5,1},{9,5},{13... | collective-permute-start | bytes 681992 | tf_op jit(solution)/shard_map/ppermute | solution.py:110
  43.4 9.5 %copy-start.4 = (s32[3,128]{1,0:T(4,128)S(1)}, s32[3,128]{1,0:T(4,128)}, u32[]{:S(2)}) copy-start(s32[3,128]{1,0:T(4,128)} %param.11) | copy-start | bytes 4612
  43.4 13.2 %slice-start.1 = ((s8[4773888]{0:T(1024)(128)(4,1)}), s8[4194304]{0:T(1024)(128)(4,1)S(1)}, s32[]{:S(2)}) async-start(s8[4773888]{0:T(1024)(128)(4,1)} %bitcast.2), calls=%async_computation.4 | async-start | bytes 8388608
  59.9 76.3 %reduce-scatter.2.cloned.1.call-start = ((), (), s32[]{:S(2)}) async-start(), calls=%async_computation.2 | async-start | bytes 2293760 | tf_op jit(solution)/shard_map/reduce_scatter | solution.py:153
  136.2 1.0 copy-start
  137.2 0.9 copy-start.1
Sparse Core Ops, SparseCore 0:
  60.0 32.9 all-reduce.1
  95.4 40.7 reduce-scatter.1

commit v2 on v0

v2 whole, which is shorter than its diff:
```python
import functools

import jax
import jax.numpy as jnp
from jax import lax
from jax.experimental import pallas as pl
from jax.experimental.pallas import tpu as pltpu
from jax.sharding import PartitionSpec as P

coarse_scale = 0.5
F32, BF16 = jnp.float32, jnp.bfloat16
MESH = pl.DeviceIdType.MESH


def dot(a, b):
    return jnp.dot(a, b, preferred_element_type=F32)


def remote(src, dst, send, recv, device):
    return pltpu.make_async_remote_copy(
        src_ref=src, dst_ref=dst, send_sem=send, recv_sem=recv, device_id=device, device_id_type=MESH)


def one_hot(row, count, ramp):
    step = ramp.shape[0]
    pieces = []
    for first in range(0, count, step):
        spot = (row - first).astype(F32).astype(BF16)
        pieces.append(jnp.where(ramp == spot, jnp.ones((), BF16), jnp.zeros((), BF16)))
    return pieces


def stack(pieces):
    return pieces[0] if len(pieces) == 1 else jnp.concatenate(pieces, axis=0)


def blocks_of(total, count, block, held):
    spare = jnp.zeros((held, total.shape[1]), F32)
    total = jnp.concatenate([total, spare], axis=0)
    return [total[j * block:j * block + held] for j in range(count)]


def kernel(spaces, reps, wide, block,
           density_hbm, up_hbm, far_hbm, down_hbm, lists, coarse_lists, out,
           density, near, far, up_ops, far_ops, down_ops, picked, ramp_ref,
           sums, right, left, gathered, coarse_here, coarse_window, coarse_sums, coarse_right, coarse_left,
           checks, full, high, low, spread,
           load_sem, window_send, window_recv, cw_send, cw_recv, ag_send, ag_recv, ck_send, ck_recv,
           rs_send, rs_recv, ls_send, ls_recv, crs_send, crs_recv, cls_send, cls_recv):
    s, z = lax.axis_index("space"), lax.axis_index("rep")
    rows, boxes = density.shape
    slots = far_ops.shape[0]
    children = up_ops.shape[0]
    parents = boxes // children
    chunks = boxes // wide
    held = sums.shape[2]
    parity = lax.rem(s, 2)
    mate = s + 1 - 2 * parity
    other = s - 1 + 2 * parity
    has_other = jnp.logical_and(other >= 0, other < spaces)

    loads = [
        pltpu.make_async_copy(src, dst, load_sem.at[i])
        for i, (src, dst) in enumerate(
            [(density_hbm, density), (up_hbm, up_ops), (far_hbm, far_ops), (down_hbm, down_ops)])
    ]
    for copy in loads:
        copy.start()

    barrier = pltpu.get_barrier_semaphore()
    for d in range(1, reps):
        pl.semaphore_signal(barrier, inc=1, device_id=(s, lax.rem(z + d, reps)), device_id_type=MESH)
    pl.semaphore_signal(barrier, inc=1, device_id=(mate, z), device_id_type=MESH)

    @pl.when(has_other)
    def _():
        pl.semaphore_signal(barrier, inc=1, device_id=(other, z), device_id_type=MESH)

    ramp_ref[...] = lax.broadcasted_iota(jnp.int32, ramp_ref.shape, 0).astype(F32).astype(BF16)
    pl.semaphore_wait(barrier, reps + has_other.astype(jnp.int32))

    to_far = remote(density_hbm, far, window_send.at[0], window_recv.at[0], (other, z))
    to_near = remote(density_hbm, near, window_send.at[1], window_recv.at[1], (mate, z))

    @pl.when(has_other)
    def _():
        to_far.start()

    to_near.start()

    @pl.when(jnp.logical_not(has_other))
    def _():
        far[...] = jnp.zeros(far.shape, BF16)
        coarse_window[:, 2 * parents:] = jnp.zeros((coarse_window.shape[0], parents), BF16)

    loads[0].wait()
    loads[1].wait()
    total = jnp.zeros((block, parents), F32)
    for child in range(0, children, 2):
        column = lax.broadcasted_iota(jnp.int32, (1, 2 * parents), 1)
        source = jnp.where(
            column < parents, column * children + child, (column - parents) * children + child + 1)
        pair = dot(density[...], stack(one_hot(source, boxes, ramp_ref[:, :2 * parents]))).astype(BF16)
        total += dot(up_ops[child], pair[:, :parents])
        total += dot(up_ops[child + 1], pair[:, parents:])
    gathered[z] = jnp.concatenate([total, jnp.zeros((held - block, parents), F32)], axis=0).astype(BF16)

    def gather_copies(buffer, send, recv):
        return [
            remote(buffer.at[z], buffer.at[z], send.at[d - 1], recv.at[d - 1], (s, lax.rem(z + d, reps)))
            for d in range(1, reps)
        ]

    up_copies = gather_copies(gathered, ag_send, ag_recv)
    for copy in up_copies:
        copy.start()

    def assemble(buffer):
        for j in range(reps):
            full[j * block:(j + 1) * block, :] = buffer[j][:block].astype(F32)
        return full[...].astype(BF16)

    own_base = boxes
    near_base = 2 * boxes * (1 - parity)
    far_base = 2 * boxes * parity
    to_near.wait_recv()

    def pick(chunk, _):
        columns = pl.ds(pl.multiple_of(chunk * wide, wide), wide)
        ramp = ramp_ref[...]
        for entry in range(slots):
            row = lists[entry:entry + 1, columns]
            values = dot(density[...], stack(one_hot(row - own_base, boxes, ramp)))
            values += dot(near[...], stack(one_hot(row - near_base, boxes, ramp)))
            picked[entry, :, columns] = values.astype(BF16)
        return 0

    first_part = chunks // 2
    lax.fori_loop(0, first_part, pick, 0)

    for copy in up_copies:
        copy.wait_recv()
    coarse_here[...] = jnp.concatenate(
        [assemble(gathered), jnp.zeros((coarse_here.shape[0] - rows, parents), BF16)], axis=0)
    coarse_window[:, :parents] = coarse_here[...]
    coarse_near = remote(
        coarse_here, coarse_window.at[:, pl.ds(parents, parents)], cw_send.at[0], cw_recv.at[0], (mate, z))
    coarse_far = remote(
        coarse_here, coarse_window.at[:, pl.ds(2 * parents, parents)], cw_send.at[1], cw_recv.at[1], (other, z))
    coarse_near.start()

    @pl.when(has_other)
    def _():
        coarse_far.start()

    lax.fori_loop(first_part, chunks, pick, 0)

    loads[2].wait()
    coarse_near.wait_recv()

    @pl.when(has_other)
    def _():
        coarse_far.wait_recv()

    total = jnp.zeros((rows, parents), F32)
    ramp = lax.broadcasted_iota(jnp.int32, (parents, parents), 0)
    for entry in range(slots):
        row = coarse_lists[entry:entry + 1, :]
        place = [
            jnp.where(ramp == row - base, 1.0, 0.0).astype(BF16)
            for base in (own_base // children, near_base // children, far_base // children)
        ]
        values = dot(coarse_window[:rows, :], stack(place))
        total += dot(far_ops[entry], values.astype(BF16))
    for j, value in enumerate(blocks_of(coarse_scale * total, reps, block, held)):
        coarse_sums[0, j] = value.astype(BF16)

    @pl.when(has_other)
    def _():
        to_far.wait_recv()

    def move_right(chunk, ways, j):
        _, buffer, _, send, recv, _, _ = ways
        return remote(buffer.at[chunk, j], buffer.at[chunk, j], send.at[chunk, j], recv.at[chunk, j], (s, z + 1))

    def move_left(chunk, ways, j):
        _, _, buffer, _, _, send, recv = ways
        return remote(buffer.at[chunk, j], buffer.at[chunk, j], send.at[chunk, j], recv.at[chunk, j], (s, z - 1))

    def forward_right(chunk, ways):
        mine, buffer = ways[0], ways[1]
        for j in reversed(range(1, reps)):
            @pl.when(j > z)
            def _(j=j):
                copy = move_right(chunk, ways, j)

                @pl.when(z > 0)
                def _():
                    copy.wait_recv()
                    buffer[chunk, j] = (buffer[chunk, j].astype(F32) + mine[chunk, j].astype(F32)).astype(BF16)

                @pl.when(z == 0)
                def _():
                    buffer[chunk, j] = mine[chunk, j]

                copy.start()

    def forward_left(chunk, ways):
        mine, buffer = ways[0], ways[2]
        for j in range(reps - 1):
            @pl.when(j < z)
            def _(j=j):
                copy = move_left(chunk, ways, j)

                @pl.when(z < reps - 1)
                def _():
                    copy.wait_recv()
                    buffer[chunk, j] = (buffer[chunk, j].astype(F32) + mine[chunk, j].astype(F32)).astype(BF16)

                @pl.when(z == reps - 1)
                def _():
                    buffer[chunk, j] = mine[chunk, j]

                copy.start()

    def finished(chunk, ways):
        mine, go_right, go_left = ways[:3]

        @pl.when(z > 0)
        def _():
            move_right(chunk, ways, z).wait_recv()

        @pl.when(z == 0)
        def _():
            go_right[chunk, z] = jnp.zeros(go_right.shape[2:], BF16)

        @pl.when(z < reps - 1)
        def _():
            move_left(chunk, ways, z).wait_recv()

        @pl.when(z == reps - 1)
        def _():
            go_left[chunk, z] = jnp.zeros(go_left.shape[2:], BF16)

        return mine[chunk, z].astype(F32) + go_right[chunk, z].astype(F32) + go_left[chunk, z].astype(F32)

    def settle(chunk, ways):
        for j in range(reps):
            @pl.when(j > z)
            def _(j=j):
                move_right(chunk, ways, j).wait_send()

            @pl.when(j < z)
            def _(j=j):
                move_left(chunk, ways, j).wait_send()

    fine_ways = (sums, right, left, rs_send, rs_recv, ls_send, ls_recv)
    coarse_ways = (coarse_sums, coarse_right, coarse_left, crs_send, crs_recv, cls_send, cls_recv)

    def step(t):
        @pl.when(t == z)
        def _():
            forward_right(0, coarse_ways)

        @pl.when(t == reps - 1 - z)
        def _():
            forward_left(0, coarse_ways)

        @pl.when(jnp.logical_and(t >= z, t - z < chunks))
        def _():
            forward_right(t - z, fine_ways)

        back = reps - 1 - z

        @pl.when(jnp.logical_and(t >= back, t - back < chunks))
        def _():
            forward_left(t - back, fine_ways)

    def translate(t, _):
        columns = pl.ds(pl.multiple_of(t * wide, wide), wide)
        ramp = ramp_ref[...]
        total = jnp.zeros((rows, wide), F32)
        for entry in range(slots):
            row = lists[entry:entry + 1, columns]
            values = dot(far[...], stack(one_hot(row - far_base, boxes, ramp)))
            values += picked[entry, :, columns].astype(F32)
            total += dot(far_ops[entry], values.astype(BF16))
        for j, value in enumerate(blocks_of(total, reps, block, held)):
            sums[t, j] = value.astype(BF16)
        step(t)
        return 0

    lax.fori_loop(0, chunks, translate, 0)

    check_copies = gather_copies(checks, ck_send, ck_recv)
    for t in range(chunks, chunks + reps - 1):
        step(t)
        if t == max(chunks, reps - 1):
            checks[z] = finished(0, coarse_ways).astype(BF16)
            for copy in check_copies:
                copy.start()

    loads[3].wait()
    for copy in check_copies:
        copy.wait_recv()
    check = assemble(checks)
    for child in range(children):
        term = dot(down_ops[child], check)
        top = term.astype(BF16)
        columns = pl.ds(child * parents, parents)
        high[:, columns] = top
        low[:, columns] = (term - top.astype(F32)).astype(BF16)

    def place(chunk, _):
        columns = pl.ds(pl.multiple_of(chunk * wide, wide), wide)
        parent = lax.broadcasted_iota(jnp.int32, (parents, wide), 0) * children
        box = lax.broadcasted_iota(jnp.int32, (parents, wide), 1) + chunk * wide
        spots = stack([
            jnp.where(parent == box - child, 1.0, 0.0).astype(BF16) for child in range(children)
        ])
        spread[:, columns] = dot(high[...], spots) + dot(low[...], spots)
        return 0

    lax.fori_loop(0, chunks, place, 0)

    def finish(chunk, _):
        columns = pl.ds(pl.multiple_of(chunk * wide, wide), wide)
        out[:, columns] = (finished(chunk, fine_ways)[:block] + spread[:, columns]).astype(BF16)
        settle(chunk, fine_ways)
        return 0

    lax.fori_loop(0, chunks, finish, 0)
    settle(0, coarse_ways)
    for copy in up_copies + check_copies + [to_near, coarse_near]:
        copy.wait_send()

    @pl.when(has_other)
    def _():
        to_far.wait_send()
        coarse_far.wait_send()


def local(spaces, reps, leaf_density, upward_ops, far_ops, downward_ops, fine_lists, coarse_lists):
    rows, boxes = leaf_density.shape
    children, block, _ = upward_ops.shape
    slots = far_ops.shape[0]
    parents = boxes // children
    wide = 256 if boxes % 256 == 0 else boxes
    chunks = boxes // wide
    held = -(-block // 16) * 16
    padded = -(-rows // 16) * 16
    vm, dma = pltpu.VMEM, pltpu.SemaphoreType.DMA
    anywhere = pl.BlockSpec(memory_space=pl.ANY)
    inside = pl.BlockSpec(memory_space=vm)
    moving = vm((chunks, reps, held, wide), BF16)
    coarse_moving = vm((1, reps, held, parents), BF16)
    return pl.pallas_call(
        functools.partial(kernel, spaces, reps, wide, block),
        out_shape=jax.ShapeDtypeStruct((block, boxes), BF16),
        in_specs=[anywhere] * 4 + [inside] * 2,
        out_specs=inside,
        scratch_shapes=[
            vm((rows, boxes), BF16), vm((rows, boxes), BF16), vm((rows, boxes), BF16),
            vm(upward_ops.shape, BF16), vm(far_ops.shape, BF16), vm(downward_ops.shape, BF16),
            vm((slots, rows, boxes), BF16), vm((min(256, boxes), wide), BF16),
            moving, moving, moving,
            vm((reps, held, parents), BF16), vm((padded, parents), BF16), vm((padded, 3 * parents), BF16),
            coarse_moving, coarse_moving, coarse_moving,
            vm((reps, held, parents), BF16), vm((rows, parents), F32),
            vm((block, boxes), BF16), vm((block, boxes), BF16), vm((block, boxes), F32),
            dma((4,)), dma((2,)), dma((2,)), dma((2,)), dma((2,)),
            dma((reps - 1,)), dma((reps - 1,)), dma((reps - 1,)), dma((reps - 1,)),
        ] + [dma((chunks, reps))] * 4 + [dma((1, reps))] * 4,
        compiler_params=pltpu.CompilerParams(
            collective_id=0, has_side_effects=True, vmem_limit_bytes=56 * 2**20),
    )(leaf_density, upward_ops, far_ops, downward_ops, fine_lists, coarse_lists)


def solution(mesh):
    return jax.shard_map(
        functools.partial(local, mesh.shape["space"], mesh.shape["rep"]),
        mesh=mesh,
        in_specs=(
            P(None, "space"),
            P(None, "rep", None),
            P("rep", None, None),
            P(None, "rep", None),
            P("rep", "space"),
            P("rep", "space"),
        ),
        out_specs=P("rep", "space"),
        check_vma=False,
    )
```

time: 191 us -> 97.1 us (0.51)
  Pallas kernels: 0 us -> 88 us
  blocking collectives: 51.4 us -> 0 us
  local copies, waits for them, and re-layouts: 59 us -> 8.04 us
  matrix products: 26.6 us -> 0 us
  starting transfers between devices: 15.3 us -> 0 us
  between operations: 14.3 us -> 0.01 us
  waiting for transfers between devices: 13.5 us -> 0 us
  other arithmetic: 9.75 us -> 0 us
    pallas_call x0 -> x1, Pallas kernels: none -> 88 us  [local(): pl.pallas_call(functools.partial(kernel, spaces, reps, wide, block), out_...]
    unnamed x1 -> x0, blocking collectives: 39.2 us -> none
    gather x6 -> x0, local copies, waits for them, and re-layouts: 35.2 us -> none  [translate(): picked = jnp.take(sources, lists[offset], axis=1)]
    dot_general x8 -> x0, matrix products: 26.6 us -> none  [the longest x6 20.2 us: translate(): jnp.dot(operators[offset], picked, preferred_element_type=jnp.float32)]
    ppermute x4 -> x0, starting transfers between devices: 14 us -> none  [the longest x2 7.78 us: extended(): before = lax.ppermute(last, axis, up)]
    ppermute x4 -> x0, waiting for transfers between devices: 13.4 us -> none  [the longest x2 13.4 us: extended(): after = lax.ppermute(initial, axis, down)]
    all_gather x1 -> x0, blocking collectives: 12.3 us -> none  [local(): stacked = lax.all_gather(up_rows, 'rep', axis=0, tiled=True)]
    ppermute x2 -> x0, local copies, waits for them, and re-layouts: 7.87 us -> none  [the longest x1 4.05 us: extended(): before = lax.ppermute(last, axis, up)]
  transfers between devices with their start and end apart: 6 -> 0, of which waited for: 1 -> 0; matrix products, arithmetic and copies ran while one was open for 68% -> 0% of each run, Pallas kernels for 0% -> 0%
where the time goes in v2:
time: 97.1 us; the launch traced here: 96.1 us
  Pallas kernels  88 us (91%)
  local copies, waits for them, and re-layouts  8.04 us (8%)
    pallas_call x1, Pallas kernels, local(): pl.pallas_call(functools.partial(kernel, spaces, reps, wide, block), out_...  88 us
    unnamed x5, local copies, waits for them, and re-layouts  8.04 us

profile of v2, /device:TPU:3, one launch (start us, length us, event | category | flops | bytes accessed | tf_op | source)
XLA Modules:
  0.0 96.1 jit_solution(5538252319851562657)
XLA Ops:
  0.0 0.0 copy-start
  0.0 4.1 %copy.7.up_hbm = bf16[8,222,888]{2,1,0:T(8,128)(2,1)} copy(bf16[8,222,888]{2,0,1:T(8,128)(2,1)} %param.7) | data formatting | bytes 6308352 | tf_op args[1]
  4.1 0.0 copy-done
  4.1 2.1 %copy.8.down_hbm = bf16[8,222,888]{2,1,0:T(8,128)(2,1)} copy(bf16[8,222,888]{2,0,1:T(8,128)(2,1)S(1)} %copy-done) | data formatting | bytes 6308352 | tf_op args[3]
  6.2 88.0 %shard_map.64 = bf16[222,1024]{1,0:T(8,128)(2,1)} custom-call(bf16[888,1024]{1,0:T(8,128)(2,1)} %density_hbm.1, bf16[8,222,888]{2,1,0:T(8,128)(2,1)} %copy.7.up_hbm, bf16[3,888,888]{2,1,0:T(8,128)(2,1)} %far_hbm.1, bf16[8,222,888]{2,1,0:T(8,128)(2,1)} %copy.8.down_hbm, s32[3,1024]{1,0:T(4,128)} %lists.1, s32[3,128]{1,0:T(4,128)} %coarse_lists.1), custom_call_target="tpu_custom_call" | custom-call | tf_op jit(solution)/shard_map/pallas_call | solution.py:357
  94.2 1.8 %copy.10 = bf16[222,1024]{1,0:T(8,128)(2,1)} copy(bf16[222,1024]{1,0:T(8,128)(2,1)} %shard_map.64) | data formatting | bytes 909312
Async XLA Ops:
  0.0 4.1 %copy-start = (bf16[8,222,888]{2,0,1:T(8,128)(2,1)S(1)}, bf16[8,222,888]{2,0,1:T(8,128)(2,1)}, u32[]{:S(2)}) copy-start(bf16[8,222,888]{2,0,1:T(8,128)(2,1)} %param.9) | copy-start | bytes 9462532

commit v3 on v2

--- a/solution.py
+++ b/solution.py
@@ -40,17 +40,17 @@
     return [total[j * block:j * block + held] for j in range(count)]
 
 
-def kernel(spaces, reps, wide, block,
+def kernel(spaces, reps, wide, piece, block,
            density_hbm, up_hbm, far_hbm, down_hbm, lists, coarse_lists, out,
-           density, near, far, up_ops, far_ops, down_ops, picked, ramp_ref,
+           density, near, far, up_raw, far_ops, down_raw, ops, wide_rows, picked, ramp_ref,
            sums, right, left, gathered, coarse_here, coarse_window, coarse_sums, coarse_right, coarse_left,
            checks, full, high, low, spread,
-           load_sem, window_send, window_recv, cw_send, cw_recv, ag_send, ag_recv, ck_send, ck_recv,
+           load_sem, window_send, window_recv, sp_send, sp_recv, cw_send, cw_recv, ag_send, ag_recv, ck_send, ck_recv,
            rs_send, rs_recv, ls_send, ls_recv, crs_send, crs_recv, cls_send, cls_recv):
     s, z = lax.axis_index("space"), lax.axis_index("rep")
     rows, boxes = density.shape
     slots = far_ops.shape[0]
-    children = up_ops.shape[0]
+    children = ops.shape[0]
     parents = boxes // children
     chunks = boxes // wide
     held = sums.shape[2]
@@ -62,7 +62,7 @@
     loads = [
         pltpu.make_async_copy(src, dst, load_sem.at[i])
         for i, (src, dst) in enumerate(
-            [(density_hbm, density), (up_hbm, up_ops), (far_hbm, far_ops), (down_hbm, down_ops)])
+            [(density_hbm, density), (up_hbm, up_raw), (far_hbm, far_ops), (down_hbm, down_raw)])
     ]
     for copy in loads:
         copy.start()
@@ -79,12 +79,24 @@
     ramp_ref[...] = lax.broadcasted_iota(jnp.int32, ramp_ref.shape, 0).astype(F32).astype(BF16)
     pl.semaphore_wait(barrier, reps + has_other.astype(jnp.int32))
 
-    to_far = remote(density_hbm, far, window_send.at[0], window_recv.at[0], (other, z))
-    to_near = remote(density_hbm, near, window_send.at[1], window_recv.at[1], (mate, z))
-
-    @pl.when(has_other)
-    def _():
-        to_far.start()
+    def share(owner):
+        return pl.ds(pl.multiple_of(owner * piece, piece), piece)
+
+    rest = pl.ds(reps * piece, boxes - reps * piece)
+    to_near = remote(density_hbm, near, window_send.at[0], window_recv.at[0], (mate, z))
+    to_share = remote(density_hbm.at[:, share(z)], far.at[:, share(z)],
+                      window_send.at[1], window_recv.at[1], (other, z))
+    to_rest = remote(density_hbm.at[:, rest], far.at[:, rest], window_send.at[2], window_recv.at[2], (other, z))
+    spread_copies = [
+        remote(far.at[:, share(z)], far.at[:, share(z)], sp_send.at[d - 1], sp_recv.at[d - 1],
+               (s, lax.rem(z + d, reps)))
+        for d in range(1, reps)
+    ]
+
+    @pl.when(has_other)
+    def _():
+        to_share.start()
+        to_rest.start()
 
     to_near.start()
 
@@ -93,16 +105,27 @@
         far[...] = jnp.zeros(far.shape, BF16)
         coarse_window[:, 2 * parents:] = jnp.zeros((coarse_window.shape[0], parents), BF16)
 
+    def by_child(raw):
+        lanes = wide_rows.shape[2]
+        for part in range(wide_rows.shape[0]):
+            low_end, high_end = part * lanes, min(rows, (part + 1) * lanes)
+            span = high_end - low_end
+            wide_rows[part, :block * children, :span] = raw[:, low_end:high_end].astype(F32)
+            for child in range(children):
+                mine = wide_rows[part, pl.ds(child, block, stride=children), :]
+                ops[child, :, low_end:high_end] = mine[:, :span].astype(BF16)
+
     loads[0].wait()
     loads[1].wait()
+    by_child(up_raw)
     total = jnp.zeros((block, parents), F32)
     for child in range(0, children, 2):
         column = lax.broadcasted_iota(jnp.int32, (1, 2 * parents), 1)
         source = jnp.where(
             column < parents, column * children + child, (column - parents) * children + child + 1)
         pair = dot(density[...], stack(one_hot(source, boxes, ramp_ref[:, :2 * parents]))).astype(BF16)
-        total += dot(up_ops[child], pair[:, :parents])
-        total += dot(up_ops[child + 1], pair[:, parents:])
+        total += dot(ops[child], pair[:, :parents])
+        total += dot(ops[child + 1], pair[:, parents:])
     gathered[z] = jnp.concatenate([total, jnp.zeros((held - block, parents), F32)], axis=0).astype(BF16)
 
     def gather_copies(buffer, send, recv):
@@ -114,6 +137,12 @@
     up_copies = gather_copies(gathered, ag_send, ag_recv)
     for copy in up_copies:
         copy.start()
+
+    @pl.when(has_other)
+    def _():
+        to_share.wait_recv()
+        for copy in spread_copies:
+            copy.start()
 
     def assemble(buffer):
         for j in range(reps):
@@ -135,7 +164,7 @@
             picked[entry, :, columns] = values.astype(BF16)
         return 0
 
-    first_part = chunks // 2
+    first_part = 1
     lax.fori_loop(0, first_part, pick, 0)
 
     for copy in up_copies:
@@ -175,10 +204,6 @@
     for j, value in enumerate(blocks_of(coarse_scale * total, reps, block, held)):
         coarse_sums[0, j] = value.astype(BF16)
 
-    @pl.when(has_other)
-    def _():
-        to_far.wait_recv()
-
     def move_right(chunk, ways, j):
         _, buffer, _, send, recv, _, _ = ways
         return remote(buffer.at[chunk, j], buffer.at[chunk, j], send.at[chunk, j], recv.at[chunk, j], (s, z + 1))
@@ -257,14 +282,17 @@
     fine_ways = (sums, right, left, rs_send, rs_recv, ls_send, ls_recv)
     coarse_ways = (coarse_sums, coarse_right, coarse_left, crs_send, crs_recv, cls_send, cls_recv)
 
+    def coarse_step(t):
+        @pl.when(t == z)
+        def _():
+            forward_right(0, coarse_ways)
+
+        @pl.when(t == reps - 1 - z)
+        def _():
+            forward_left(0, coarse_ways)
+
     def step(t):
-        @pl.when(t == z)
-        def _():
-            forward_right(0, coarse_ways)
-
-        @pl.when(t == reps - 1 - z)
-        def _():
-            forward_left(0, coarse_ways)
+        coarse_step(t + 1)
 
         @pl.when(jnp.logical_and(t >= z, t - z < chunks))
         def _():
@@ -290,6 +318,14 @@
         step(t)
         return 0
 
+    coarse_step(0)
+
+    @pl.when(has_other)
+    def _():
+        to_rest.wait_recv()
+        for copy in spread_copies:
+            copy.wait_recv()
+
     lax.fori_loop(0, chunks, translate, 0)
 
     check_copies = gather_copies(checks, ck_send, ck_recv)
@@ -299,13 +335,14 @@
             checks[z] = finished(0, coarse_ways).astype(BF16)
             for copy in check_copies:
                 copy.start()
-
-    loads[3].wait()
+            loads[3].wait()
+            by_child(down_raw)
+
     for copy in check_copies:
         copy.wait_recv()
     check = assemble(checks)
     for child in range(children):
-        term = dot(down_ops[child], check)
+        term = dot(ops[child], check)
         top = term.astype(BF16)
         columns = pl.ds(child * parents, parents)
         high[:, columns] = top
@@ -336,7 +373,10 @@
 
     @pl.when(has_other)
     def _():
-        to_far.wait_send()
+        to_share.wait_send()
+        to_rest.wait_send()
+        for copy in spread_copies:
+            copy.wait_send()
         coarse_far.wait_send()
 
 
@@ -347,6 +387,8 @@
     parents = boxes // children
     wide = 256 if boxes % 256 == 0 else boxes
     chunks = boxes // wide
+    piece = 128 if boxes >= 256 * reps else boxes // (2 * reps)
+    by_row = [ops.transpose(1, 0, 2).reshape(block * children, rows) for ops in (upward_ops, downward_ops)]
     held = -(-block // 16) * 16
     padded = -(-rows // 16) * 16
     vm, dma = pltpu.VMEM, pltpu.SemaphoreType.DMA
@@ -355,25 +397,26 @@
     moving = vm((chunks, reps, held, wide), BF16)
     coarse_moving = vm((1, reps, held, parents), BF16)
     return pl.pallas_call(
-        functools.partial(kernel, spaces, reps, wide, block),
+        functools.partial(kernel, spaces, reps, wide, piece, block),
         out_shape=jax.ShapeDtypeStruct((block, boxes), BF16),
         in_specs=[anywhere] * 4 + [inside] * 2,
         out_specs=inside,
         scratch_shapes=[
             vm((rows, boxes), BF16), vm((rows, boxes), BF16), vm((rows, boxes), BF16),
-            vm(upward_ops.shape, BF16), vm(far_ops.shape, BF16), vm(downward_ops.shape, BF16),
+            vm((block * children, rows), BF16), vm(far_ops.shape, BF16), vm((block * children, rows), BF16),
+            vm(upward_ops.shape, BF16), vm((-(-rows // 128), held * children, 128), F32),
             vm((slots, rows, boxes), BF16), vm((min(256, boxes), wide), BF16),
             moving, moving, moving,
             vm((reps, held, parents), BF16), vm((padded, parents), BF16), vm((padded, 3 * parents), BF16),
             coarse_moving, coarse_moving, coarse_moving,
             vm((reps, held, parents), BF16), vm((rows, parents), F32),
             vm((block, boxes), BF16), vm((block, boxes), BF16), vm((block, boxes), F32),
-            dma((4,)), dma((2,)), dma((2,)), dma((2,)), dma((2,)),
+            dma((4,)), dma((3,)), dma((3,)), dma((reps - 1,)), dma((reps - 1,)), dma((2,)), dma((2,)),
             dma((reps - 1,)), dma((reps - 1,)), dma((reps - 1,)), dma((reps - 1,)),
         ] + [dma((chunks, reps))] * 4 + [dma((1, reps))] * 4,
         compiler_params=pltpu.CompilerParams(
             collective_id=0, has_side_effects=True, vmem_limit_bytes=56 * 2**20),
-    )(leaf_density, upward_ops, far_ops, downward_ops, fine_lists, coarse_lists)
+    )(leaf_density, by_row[0], far_ops, by_row[1], fine_lists, coarse_lists)
 
 
 def solution(mesh):

time: 97.1 us -> 86.7 us (0.89)
  local copies, waits for them, and re-layouts: 8.04 us -> 1.82 us
  Pallas kernels: 88 us -> 84.6 us
    unnamed x5 -> x1, local copies, waits for them, and re-layouts: 8.04 us -> 1.82 us
    pallas_call x1, Pallas kernels: 88 us -> 84.6 us  [local(): pl.pallas_call(functools.partial(kernel, spaces, reps, wide, piece, block...]
where the time goes in v3:
time: 86.7 us; the launch traced here: 86.4 us
  Pallas kernels  84.6 us (98%)
  local copies, waits for them, and re-layouts  1.82 us (2%)
    pallas_call x1, Pallas kernels, local(): pl.pallas_call(functools.partial(kernel, spaces, reps, wide, piece, block...  84.6 us
    unnamed x1, local copies, waits for them, and re-layouts  1.82 us

profile of v3, /device:TPU:3, one launch (start us, length us, event | category | flops | bytes accessed | tf_op | source)
XLA Modules:
  0.0 86.4 jit_solution(11131793307430783472)
XLA Ops:
  0.0 84.6 %shard_map.64 = bf16[222,1024]{1,0:T(8,128)(2,1)} custom-call(bf16[888,1024]{1,0:T(8,128)(2,1)} %density_hbm.1, bf16[1776,888]{1,0:T(8,128)(2,1)} %bitcast.6, bf16[3,888,888]{2,1,0:T(8,128)(2,1)} %far_hbm.1, bf16[1776,888]{1,0:T(8,128)(2,1)} %bitcast.7, s32[3,1024]{1,0:T(4,128)} %lists.1, s32[3,128]{1,0:T(4,128)} %coarse_lists.1), custom_call_target="tpu_custom_call" | custom-call | tf_op jit(solution)/shard_map/pallas_call | solution.py:399
  84.6 1.8 %copy.8 = bf16[222,1024]{1,0:T(8,128)(2,1)} copy(bf16[222,1024]{1,0:T(8,128)(2,1)} %shard_map.64) | data formatting | bytes 909312

commit v4 on v3

--- a/solution.py
+++ b/solution.py
@@ -40,15 +40,35 @@
     return [total[j * block:j * block + held] for j in range(count)]
 
 
+def by_child(tall, children):
+    groups, lanes = tall.shape[0] // (children * children), tall.shape[1]
+    cube = tall.reshape(groups, children, children, lanes)
+    parts = [cube[:, i] for i in range(children)]
+    child = lax.broadcasted_iota(jnp.int32, parts[0].shape, 1)
+    bit = children // 2
+    while bit:
+        clear = (child & bit) == 0
+        moved = list(parts)
+        for i in range(children):
+            if i & bit == 0:
+                first, second = parts[i], parts[i | bit]
+                moved[i] = jnp.where(clear, first, pltpu.roll(second, bit, 1))
+                moved[i | bit] = jnp.where(clear, pltpu.roll(first, children - bit, 1), second)
+        parts = moved
+        bit //= 2
+    return [part.reshape(groups * children, lanes) for part in parts]
+
+
 def kernel(spaces, reps, wide, piece, block,
            density_hbm, up_hbm, far_hbm, down_hbm, lists, coarse_lists, out,
-           density, near, far, up_raw, far_ops, down_raw, ops, wide_rows, picked, ramp_ref,
+           window, up_raw, far_ops, down_raw, ops, picked, ramp_ref,
            sums, right, left, gathered, coarse_here, coarse_window, coarse_sums, coarse_right, coarse_left,
            checks, full, high, low, spread,
            load_sem, window_send, window_recv, sp_send, sp_recv, cw_send, cw_recv, ag_send, ag_recv, ck_send, ck_recv,
            rs_send, rs_recv, ls_send, ls_recv, crs_send, crs_recv, cls_send, cls_recv):
     s, z = lax.axis_index("space"), lax.axis_index("rep")
-    rows, boxes = density.shape
+    rows, boxes = density_hbm.shape
+    density, near, far = (window.at[:, pl.ds(i * boxes, boxes)] for i in range(3))
     slots = far_ops.shape[0]
     children = ops.shape[0]
     parents = boxes // children
@@ -102,22 +122,24 @@
 
     @pl.when(jnp.logical_not(has_other))
     def _():
-        far[...] = jnp.zeros(far.shape, BF16)
+        far[...] = jnp.zeros((rows, boxes), BF16)
         coarse_window[:, 2 * parents:] = jnp.zeros((coarse_window.shape[0], parents), BF16)
 
-    def by_child(raw):
-        lanes = wide_rows.shape[2]
-        for part in range(wide_rows.shape[0]):
-            low_end, high_end = part * lanes, min(rows, (part + 1) * lanes)
-            span = high_end - low_end
-            wide_rows[part, :block * children, :span] = raw[:, low_end:high_end].astype(F32)
-            for child in range(children):
-                mine = wide_rows[part, pl.ds(child, block, stride=children), :]
-                ops[child, :, low_end:high_end] = mine[:, :span].astype(BF16)
+    def put_up():
+        lanes = 128 if rows > 128 else rows
+        for first in range(0, rows, lanes):
+            span = min(lanes, rows - first)
+            columns = slice(first, first + span)
+            tall = jnp.concatenate(
+                [up_raw[:, columns].astype(F32), jnp.zeros((children * (held - block), span), F32)], axis=0)
+            if span < lanes:
+                tall = jnp.concatenate([tall, jnp.zeros((tall.shape[0], lanes - span), F32)], axis=1)
+            for child, value in enumerate(by_child(tall, children)):
+                ops[child, :, columns] = value[:block, :span].astype(BF16)
 
     loads[0].wait()
     loads[1].wait()
-    by_child(up_raw)
+    put_up()
     total = jnp.zeros((block, parents), F32)
     for child in range(0, children, 2):
         column = lax.broadcasted_iota(jnp.int32, (1, 2 * parents), 1)
@@ -157,11 +179,11 @@
     def pick(chunk, _):
         columns = pl.ds(pl.multiple_of(chunk * wide, wide), wide)
         ramp = ramp_ref[...]
+        row = jnp.concatenate([lists[entry:entry + 1, columns] for entry in range(slots)], axis=1)
+        spots = one_hot(row - own_base, boxes, ramp) + one_hot(row - near_base, boxes, ramp)
+        values = dot(window[:, :2 * boxes], stack(spots))
         for entry in range(slots):
-            row = lists[entry:entry + 1, columns]
-            values = dot(density[...], stack(one_hot(row - own_base, boxes, ramp)))
-            values += dot(near[...], stack(one_hot(row - near_base, boxes, ramp)))
-            picked[entry, :, columns] = values.astype(BF16)
+            picked[entry, :, columns] = values[:, entry * wide:(entry + 1) * wide].astype(BF16)
         return 0
 
     first_part = 1
@@ -192,15 +214,15 @@
         coarse_far.wait_recv()
 
     total = jnp.zeros((rows, parents), F32)
-    ramp = lax.broadcasted_iota(jnp.int32, (parents, parents), 0)
+    row = jnp.concatenate([coarse_lists[entry:entry + 1, :] for entry in range(slots)], axis=1)
+    ramp = lax.broadcasted_iota(jnp.int32, (parents, slots * parents), 0)
+    place = [
+        jnp.where(ramp == row - base, 1.0, 0.0).astype(BF16)
+        for base in (own_base // children, near_base // children, far_base // children)
+    ]
+    values = dot(coarse_window[:rows, :], stack(place)).astype(BF16)
     for entry in range(slots):
-        row = coarse_lists[entry:entry + 1, :]
-        place = [
-            jnp.where(ramp == row - base, 1.0, 0.0).astype(BF16)
-            for base in (own_base // children, near_base // children, far_base // children)
-        ]
-        values = dot(coarse_window[:rows, :], stack(place))
-        total += dot(far_ops[entry], values.astype(BF16))
+        total += dot(far_ops[entry], values[:, entry * parents:(entry + 1) * parents])
     for j, value in enumerate(blocks_of(coarse_scale * total, reps, block, held)):
         coarse_sums[0, j] = value.astype(BF16)
 
@@ -308,11 +330,11 @@
         columns = pl.ds(pl.multiple_of(t * wide, wide), wide)
         ramp = ramp_ref[...]
         total = jnp.zeros((rows, wide), F32)
+        row = jnp.concatenate([lists[entry:entry + 1, columns] for entry in range(slots)], axis=1)
+        values = dot(window[:, 2 * boxes:], stack(one_hot(row - far_base, boxes, ramp)))
         for entry in range(slots):
-            row = lists[entry:entry + 1, columns]
-            values = dot(far[...], stack(one_hot(row - far_base, boxes, ramp)))
-            values += picked[entry, :, columns].astype(F32)
-            total += dot(far_ops[entry], values.astype(BF16))
+            source = values[:, entry * wide:(entry + 1) * wide] + picked[entry, :, columns].astype(F32)
+            total += dot(far_ops[entry], source.astype(BF16))
         for j, value in enumerate(blocks_of(total, reps, block, held)):
             sums[t, j] = value.astype(BF16)
         step(t)
@@ -335,18 +357,18 @@
             checks[z] = finished(0, coarse_ways).astype(BF16)
             for copy in check_copies:
                 copy.start()
-            loads[3].wait()
-            by_child(down_raw)
 
     for copy in check_copies:
         copy.wait_recv()
     check = assemble(checks)
-    for child in range(children):
-        term = dot(ops[child], check)
-        top = term.astype(BF16)
+    loads[3].wait()
+    term = jnp.concatenate(
+        [dot(down_raw[...], check), jnp.zeros((children * (held - block), parents), F32)], axis=0)
+    for child, value in enumerate(by_child(term, children)):
+        top = value[:block].astype(BF16)
         columns = pl.ds(child * parents, parents)
         high[:, columns] = top
-        low[:, columns] = (term - top.astype(F32)).astype(BF16)
+        low[:, columns] = (value[:block] - top.astype(F32)).astype(BF16)
 
     def place(chunk, _):
         columns = pl.ds(pl.multiple_of(chunk * wide, wide), wide)
@@ -402,10 +424,10 @@
         in_specs=[anywhere] * 4 + [inside] * 2,
         out_specs=inside,
         scratch_shapes=[
-            vm((rows, boxes), BF16), vm((rows, boxes), BF16), vm((rows, boxes), BF16),
+            vm((rows, 3 * boxes), BF16),
             vm((block * children, rows), BF16), vm(far_ops.shape, BF16), vm((block * children, rows), BF16),
-            vm(upward_ops.shape, BF16), vm((-(-rows // 128), held * children, 128), F32),
-            vm((slots, rows, boxes), BF16), vm((min(256, boxes), wide), BF16),
+            vm(upward_ops.shape, BF16),
+            vm((slots, rows, boxes), BF16), vm((min(256, boxes), slots * wide), BF16),
             moving, moving, moving,
             vm((reps, held, parents), BF16), vm((padded, parents), BF16), vm((padded, 3 * parents), BF16),
             coarse_moving, coarse_moving, coarse_moving,

time: 86.7 us -> 87.1 us (level)
  no operation moved by 1% of the time
where the time goes in v4:
time: 87.1 us; the launch traced here: 86.8 us
  Pallas kernels  85 us (98%)
  local copies, waits for them, and re-layouts  1.82 us (2%)
    pallas_call x1, Pallas kernels, local(): pl.pallas_call(functools.partial(kernel, spaces, reps, wide, piece, block...  85 us
    unnamed x1, local copies, waits for them, and re-layouts  1.82 us

profile of v4, /device:TPU:3, one launch (start us, length us, event | category | flops | bytes accessed | tf_op | source)
XLA Modules:
  0.0 86.8 jit_solution(11549214757264041786)
XLA Ops:
  0.0 85.0 %shard_map.64 = bf16[222,1024]{1,0:T(8,128)(2,1)} custom-call(bf16[888,1024]{1,0:T(8,128)(2,1)} %density_hbm.1, bf16[1776,888]{1,0:T(8,128)(2,1)} %bitcast.6, bf16[3,888,888]{2,1,0:T(8,128)(2,1)} %far_hbm.1, bf16[1776,888]{1,0:T(8,128)(2,1)} %bitcast.7, s32[3,1024]{1,0:T(4,128)} %lists.1, s32[3,128]{1,0:T(4,128)} %coarse_lists.1), custom_call_target="tpu_custom_call" | custom-call | tf_op jit(solution)/shard_map/pallas_call | solution.py:421
  85.0 1.8 %copy.8 = bf16[222,1024]{1,0:T(8,128)(2,1)} copy(bf16[222,1024]{1,0:T(8,128)(2,1)} %shard_map.64) | data formatting | bytes 909312

commit v5 on v4

--- a/solution.py
+++ b/solution.py
@@ -102,7 +102,16 @@
     def share(owner):
         return pl.ds(pl.multiple_of(owner * piece, piece), piece)
 
+    def is_helped(target):
+        return jnp.logical_and(lax.rem(target, 8) != 2, lax.rem(target, 8) != 5)
+
+    helped = jnp.logical_and(has_other, is_helped(s))
+    helps = jnp.logical_and(has_other, is_helped(other))
+    whole_in = jnp.logical_and(has_other, jnp.logical_not(is_helped(s)))
+    whole_out = jnp.logical_and(has_other, jnp.logical_not(is_helped(other)))
+    first = pl.ds(0, reps * piece)
     rest = pl.ds(reps * piece, boxes - reps * piece)
+    to_first = remote(density_hbm.at[:, first], far.at[:, first], window_send.at[3], window_recv.at[3], (other, z))
     to_near = remote(density_hbm, near, window_send.at[0], window_recv.at[0], (mate, z))
     to_share = remote(density_hbm.at[:, share(z)], far.at[:, share(z)],
                       window_send.at[1], window_recv.at[1], (other, z))
@@ -113,10 +122,13 @@
         for d in range(1, reps)
     ]
 
-    @pl.when(has_other)
+    @pl.when(helps)
     def _():
         to_share.start()
-        to_rest.start()
+
+    @pl.when(whole_out)
+    def _():
+        to_first.start()
 
     to_near.start()
 
@@ -162,6 +174,10 @@
 
     @pl.when(has_other)
     def _():
+        to_rest.start()
+
+    @pl.when(helped)
+    def _():
         to_share.wait_recv()
         for copy in spread_copies:
             copy.start()
@@ -174,6 +190,7 @@
     own_base = boxes
     near_base = 2 * boxes * (1 - parity)
     far_base = 2 * boxes * parity
+    head = reps * piece
     to_near.wait_recv()
 
     def pick(chunk, _):
@@ -331,7 +348,7 @@
         ramp = ramp_ref[...]
         total = jnp.zeros((rows, wide), F32)
         row = jnp.concatenate([lists[entry:entry + 1, columns] for entry in range(slots)], axis=1)
-        values = dot(window[:, 2 * boxes:], stack(one_hot(row - far_base, boxes, ramp)))
+        values = dot(window[:, 2 * boxes + head:], stack(one_hot(row - far_base - head, boxes - head, ramp)))
         for entry in range(slots):
             source = values[:, entry * wide:(entry + 1) * wide] + picked[entry, :, columns].astype(F32)
             total += dot(far_ops[entry], source.astype(BF16))
@@ -342,11 +359,29 @@
 
     coarse_step(0)
 
-    @pl.when(has_other)
-    def _():
-        to_rest.wait_recv()
+    @pl.when(helped)
+    def _():
         for copy in spread_copies:
             copy.wait_recv()
+
+    @pl.when(whole_in)
+    def _():
+        to_first.wait_recv()
+
+    def pick_first(chunk, _):
+        columns = pl.ds(pl.multiple_of(chunk * wide, wide), wide)
+        row = jnp.concatenate([lists[entry:entry + 1, columns] for entry in range(slots)], axis=1)
+        values = dot(window[:, 2 * boxes:2 * boxes + head], stack(one_hot(row - far_base, head, ramp_ref[...])))
+        for entry in range(slots):
+            part = values[:, entry * wide:(entry + 1) * wide] + picked[entry, :, columns].astype(F32)
+            picked[entry, :, columns] = part.astype(BF16)
+        return 0
+
+    lax.fori_loop(0, chunks, pick_first, 0)
+
+    @pl.when(has_other)
+    def _():
+        to_rest.wait_recv()
 
     lax.fori_loop(0, chunks, translate, 0)
 
@@ -395,10 +430,23 @@
 
     @pl.when(has_other)
     def _():
+        to_rest.wait_send()
+
+    @pl.when(helps)
+    def _():
         to_share.wait_send()
-        to_rest.wait_send()
+
+    @pl.when(whole_out)
+    def _():
+        to_first.wait_send()
+
+    @pl.when(helped)
+    def _():
         for copy in spread_copies:
             copy.wait_send()
+
+    @pl.when(has_other)
+    def _():
         coarse_far.wait_send()
 
 
@@ -433,7 +481,7 @@
             coarse_moving, coarse_moving, coarse_moving,
             vm((reps, held, parents), BF16), vm((rows, parents), F32),
             vm((block, boxes), BF16), vm((block, boxes), BF16), vm((block, boxes), F32),
-            dma((4,)), dma((3,)), dma((3,)), dma((reps - 1,)), dma((reps - 1,)), dma((2,)), dma((2,)),
+            dma((4,)), dma((4,)), dma((4,)), dma((reps - 1,)), dma((reps - 1,)), dma((2,)), dma((2,)),
             dma((reps - 1,)), dma((reps - 1,)), dma((reps - 1,)), dma((reps - 1,)),
         ] + [dma((chunks, reps))] * 4 + [dma((1, reps))] * 4,
         compiler_params=pltpu.CompilerParams(

time: 87.1 us -> 84.8 us (0.974); the launches traced: 86.8 us -> 83.6 us
  Pallas kernels: 85 us -> 81.8 us
    pallas_call x1, Pallas kernels: 85 us -> 81.8 us  [local(): pl.pallas_call(functools.partial(kernel, spaces, reps, wide, piece, block...]
where the time goes in v5:
time: 84.8 us; the launch traced here: 83.6 us
  Pallas kernels  81.8 us (96%)
  local copies, waits for them, and re-layouts  1.82 us (2%)
    pallas_call x1, Pallas kernels, local(): pl.pallas_call(functools.partial(kernel, spaces, reps, wide, piece, block...  81.8 us
    unnamed x1, local copies, waits for them, and re-layouts  1.82 us

profile of v5, /device:TPU:3, one launch (start us, length us, event | category | flops | bytes accessed | tf_op | source)
XLA Modules:
  0.0 83.6 jit_solution(9374659419897766971)
XLA Ops:
  0.0 81.8 %shard_map.64 = bf16[222,1024]{1,0:T(8,128)(2,1)} custom-call(bf16[888,1024]{1,0:T(8,128)(2,1)} %density_hbm.1, bf16[1776,888]{1,0:T(8,128)(2,1)} %bitcast.6, bf16[3,888,888]{2,1,0:T(8,128)(2,1)} %far_hbm.1, bf16[1776,888]{1,0:T(8,128)(2,1)} %bitcast.7, s32[3,1024]{1,0:T(4,128)} %lists.1, s32[3,128]{1,0:T(4,128)} %coarse_lists.1), custom_call_target="tpu_custom_call" | custom-call | tf_op jit(solution)/shard_map/pallas_call | solution.py:469
  81.8 1.8 %copy.8 = bf16[222,1024]{1,0:T(8,128)(2,1)} copy(bf16[222,1024]{1,0:T(8,128)(2,1)} %shard_map.64) | data formatting | bytes 909312

commit v6 on v5

--- a/solution.py
+++ b/solution.py
@@ -223,25 +223,25 @@
 
     lax.fori_loop(first_part, chunks, pick, 0)
 
-    loads[2].wait()
-    coarse_near.wait_recv()
-
-    @pl.when(has_other)
-    def _():
-        coarse_far.wait_recv()
-
-    total = jnp.zeros((rows, parents), F32)
-    row = jnp.concatenate([coarse_lists[entry:entry + 1, :] for entry in range(slots)], axis=1)
-    ramp = lax.broadcasted_iota(jnp.int32, (parents, slots * parents), 0)
-    place = [
-        jnp.where(ramp == row - base, 1.0, 0.0).astype(BF16)
-        for base in (own_base // children, near_base // children, far_base // children)
-    ]
-    values = dot(coarse_window[:rows, :], stack(place)).astype(BF16)
-    for entry in range(slots):
-        total += dot(far_ops[entry], values[:, entry * parents:(entry + 1) * parents])
-    for j, value in enumerate(blocks_of(coarse_scale * total, reps, block, held)):
-        coarse_sums[0, j] = value.astype(BF16)
+    def coarse():
+        coarse_near.wait_recv()
+
+        @pl.when(has_other)
+        def _():
+            coarse_far.wait_recv()
+
+        total = jnp.zeros((rows, parents), F32)
+        row = jnp.concatenate([coarse_lists[entry:entry + 1, :] for entry in range(slots)], axis=1)
+        ramp = lax.broadcasted_iota(jnp.int32, (parents, slots * parents), 0)
+        place = [
+            jnp.where(ramp == row - base, 1.0, 0.0).astype(BF16)
+            for base in (own_base // children, near_base // children, far_base // children)
+        ]
+        values = dot(coarse_window[:rows, :], stack(place)).astype(BF16)
+        for entry in range(slots):
+            total += dot(far_ops[entry], values[:, entry * parents:(entry + 1) * parents])
+        for j, value in enumerate(blocks_of(coarse_scale * total, reps, block, held)):
+            coarse_sums[0, j] = value.astype(BF16)
 
     def move_right(chunk, ways, j):
         _, buffer, _, send, recv, _, _ = ways
@@ -331,7 +331,7 @@
             forward_left(0, coarse_ways)
 
     def step(t):
-        coarse_step(t + 1)
+        coarse_step(t - 1)
 
         @pl.when(jnp.logical_and(t >= z, t - z < chunks))
         def _():
@@ -344,6 +344,10 @@
             forward_left(t - back, fine_ways)
 
     def translate(t, _):
+        @pl.when(whole_in)
+        def _():
+            pick_first(t, 0)
+
         columns = pl.ds(pl.multiple_of(t * wide, wide), wide)
         ramp = ramp_ref[...]
         total = jnp.zeros((rows, wide), F32)
@@ -355,14 +359,14 @@
         for j, value in enumerate(blocks_of(total, reps, block, held)):
             sums[t, j] = value.astype(BF16)
         step(t)
+
+        @pl.when(jnp.logical_and(t == 0, jnp.logical_not(helped)))
+        def _():
+            coarse()
+
         return 0
 
-    coarse_step(0)
-
-    @pl.when(helped)
-    def _():
-        for copy in spread_copies:
-            copy.wait_recv()
+    loads[2].wait()
 
     @pl.when(whole_in)
     def _():
@@ -377,7 +381,12 @@
             picked[entry, :, columns] = part.astype(BF16)
         return 0
 
-    lax.fori_loop(0, chunks, pick_first, 0)
+    @pl.when(helped)
+    def _():
+        coarse()
+        for copy in spread_copies:
+            copy.wait_recv()
+        lax.fori_loop(0, chunks, pick_first, 0)
 
     @pl.when(has_other)
     def _():

time: 84.8 us -> 83.9 us (0.989); the launches traced: 83.6 us -> 83.7 us
  no operation moved by 1% of the time
where the time goes in v6:
time: 83.9 us; the launch traced here: 83.7 us
  Pallas kernels  81.9 us (98%)
  local copies, waits for them, and re-layouts  1.82 us (2%)
    pallas_call x1, Pallas kernels, local(): pl.pallas_call(functools.partial(kernel, spaces, reps, wide, piece, block...  81.9 us
    unnamed x1, local copies, waits for them, and re-layouts  1.82 us

profile of v6, /device:TPU:3, one launch (start us, length us, event | category | flops | bytes accessed | tf_op | source)
XLA Modules:
  0.0 83.7 jit_solution(10215521070831299524)
XLA Ops:
  0.0 81.9 %shard_map.64 = bf16[222,1024]{1,0:T(8,128)(2,1)} custom-call(bf16[888,1024]{1,0:T(8,128)(2,1)} %density_hbm.1, bf16[1776,888]{1,0:T(8,128)(2,1)} %bitcast.6, bf16[3,888,888]{2,1,0:T(8,128)(2,1)} %far_hbm.1, bf16[1776,888]{1,0:T(8,128)(2,1)} %bitcast.7, s32[3,1024]{1,0:T(4,128)} %lists.1, s32[3,128]{1,0:T(4,128)} %coarse_lists.1), custom_call_target="tpu_custom_call" | custom-call | tf_op jit(solution)/shard_map/pallas_call | solution.py:478
  81.9 1.8 %copy.8 = bf16[222,1024]{1,0:T(8,128)(2,1)} copy(bf16[222,1024]{1,0:T(8,128)(2,1)} %shard_map.64) | data formatting | bytes 909312
